TPU v7x, 256 devices: a whole 4x4x8 slice. The times are simulated.
256 devices in a mesh: row: 32 (over z, y), col: 8 (over x, core).
Axes of the slice: x: 4, y: 4, z: 8, core: 2. Of those that a mesh axis runs over, the one named last changes fastest.
Arguments:
- jacobian: float32 [512, 16384], P('col', 'row'), may hold values from -0.25 to 0.25
- residual: float32 [512], P('col'), may hold values from -240 to 240
- normal_prior: float32 [16384, 16384], P('row', 'col'), may hold values from -0.3 to 0.3
Outputs:
- normal_damped: float32 [16384, 16384], P('row', 'col')
- gradient: float32 [16384], P('row')
All inputs are finite; a program needn't handle non-finite values.
Results may differ from a plain program's by a relative error of at most 0.00008.
Values sent between devices are 32-bit elements; how exact they have to be, the bound alone decides.
No kernel may reach another device: no remote copies, remote signals or barrier semaphores. Data moves between devices by JAX's collectives and lax.ppermute only.
A program may use at most 64 MiB of HBM per device.

v0:
```python
import jax
import jax.numpy as jnp
from jax import lax
from jax.sharding import PartitionSpec as P

damping_scale = 0.2


def broadcast(shard, axis, root):
    mine = lax.axis_index(axis) == root
    return lax.psum(jnp.where(mine, shard, jnp.zeros_like(shard)), axis)


def per_device(jacobian, residual, normal_prior):
    highest = lax.Precision.HIGHEST
    group_count = lax.axis_size("row") // lax.axis_size("col")
    col_index = lax.axis_index("col")
    width = jacobian.shape[1]
    total_rows = residual.shape[0] * lax.axis_size("col")
    partial_value = lax.dot_general(
        jacobian,
        residual,
        (((0,), (0,)), ((), ())),
        precision=highest,
        preferred_element_type=jnp.float32,
    )
    gradient, squares = lax.psum((partial_value, jnp.sum(residual * residual)), "col")
    damping = damping_scale * jnp.sqrt(squares / total_rows + 1e-06)
    column_panel = lax.all_gather(jacobian, "col", axis=0, tiled=True)
    received = []
    for offset in range(group_count):
        received.append(broadcast(column_panel, "row", col_index * group_count + offset))
    partner_cols = jnp.concatenate(received, axis=1)
    normal_block = lax.dot_general(
        column_panel,
        partner_cols,
        (((0,), (0,)), ((), ())),
        precision=highest,
        preferred_element_type=jnp.float32,
    )
    row_ids = lax.axis_index("row") * width + lax.broadcasted_iota(jnp.int32, normal_block.shape, 0)
    col_ids = col_index * normal_block.shape[1] + lax.broadcasted_iota(
        jnp.int32, normal_block.shape, 1
    )
    on_diagonal = (row_ids == col_ids).astype(jnp.float32)
    damped = normal_prior + normal_block * (1.0 + damping * on_diagonal)
    return (damped, gradient)


def solution(mesh):
    return jax.shard_map(
        per_device,
        mesh=mesh,
        in_specs=(P("col", "row"), P("col"), P("row", "col")),
        out_specs=(P("row", "col"), P("row")),
        check_vma=False,
    )
```

profile of v0, /device:TPU:2, one launch (start us, length us, event | category | flops | bytes accessed | tf_op | source)
XLA Modules:
  0.0 231.1 jit_solution(17461042579569981360)
XLA Ops:
  7.2 0.0 all-gather.2.cloned.1.call-start
  7.2 0.7 all-gather.2.cloned.1.call-update
  7.9 0.0 all-reduce.4.cloned.1.call-start
  8.0 0.0 copy-start.2
  8.0 0.0 copy-start.1
  8.0 29.1 %all-gather.2.cloned.1.call-done = f32[512,512]{1,0:T(8,128)} async-done(((f32[64,512]{1,0:T(8,128)}), f32[512,512]{1,0:T(8,128)}) %all-gather.2.cloned.1.call-update) | async-done | bytes 1048592 | tf_op jit(solution)/shard_map/all_gather | solution.py:29
  37.1 3.5 %broadcast_select_fusion.3 = (f32[512,512]{1,0:T(8,128)}, f32[512,512]{1,0:T(8,128)}, f32[512,512]{1,0:T(8,128)}, f32[512,512]{1,0:T(8,128)}) fusion(f32[512,512]{1,0:T(8,128)} %all-gather.2.cloned.1.call-done, pred[]{:T(512)S(6)} %eq.15, pred[]{:T(512)S(6)} %eq.18, pred[]{:T(512)S(6)} %eq.17, pred[]{:T(512)S(6)} %eq.16), kind=kLoop, calls=%fused_computation.13 | loop fusion | flops 1048576 | bytes 5242884 | tf_op jit(solution)/shard_map/jit(_where)/select_n | solution.py:11
  40.5 0.0 all-reduce.4.cloned.1.call-update
  40.6 0.0 copy-done.2
  40.6 0.6 multiply_reduce_fusion
  41.2 0.0 copy-done.1
  41.2 0.2 fusion.11
  41.4 12.8 %all-reduce.1 = (f32[]{:T(128)}, f32[512]{0:T(512)}) all-reduce(f32[]{:T(128)} %multiply_reduce_fusion, f32[512]{0:T(512)S(1)} %bitcast.10), channel_id=1, replica_groups=mesh['row'=32,'col'=8] {'col'}, use_global_device_ids=true, to_apply=%region_5.6 | all-reduce | flops 513 | bytes 4104 | tf_op jit(solution)/shard_map/psum | solution.py:27
  54.8 0.0 copy-start
  54.8 5.4 %copy.5 = f32[512,2048]{0,1:T(8,128)} copy(f32[512,2048]{1,0:T(8,128)} %param.5) | data formatting | bytes 8388608 | tf_op args[2]
  60.3 146.8 %all-reduce.4.cloned.1.call-done = (f32[512,512]{1,0:T(8,128)}, f32[512,512]{1,0:T(8,128)}, f32[512,512]{1,0:T(8,128)}, f32[512,512]{1,0:T(8,128)}) async-done(((f32[512,512]{1,0:T(8,128)}, f32[512,512]{1,0:T(8,128)}, f32[512,512]{1,0:T(8,128)}, f32[512,512]{1,0:T(8,128)}), (f32[512,512]{1,0:T(8,128)}, f32[512,512]{1,0:T(8,128)}, f32[512,512]{1,0:T(8,128)}, ...) | async-done | bytes 4194320 | tf_op jit(solution)/shard_map/psum | solution.py:11
  207.1 0.0 copy-done
  207.1 11.8 %fusion.8 = f32[512,2048]{0,1:T(8,128)} fusion(f32[512,2048]{0,1:T(8,128)} %copy.5, f32[512,512]{1,0:T(8,128)S(1)} %copy-done, f32[512,512]{1,0:T(8,128)} %get-tuple-element.4, f32[512,512]{1,0:T(8,128)} %get-tuple-element.5, f32[512,512]{1,0:T(8,128)} %get-tuple-element.6, f32[512,512]{1,0:T(8,128)} %get-tuple-element.7, f32[]{:T(128)S(6)} %mul_shard_map.3, ...), kind=kOutput, calls=%fused_computation.9 | convolution fusion | flops 6450839552 | bytes 13641732 | tf_op jit(solution)/shard_map/dot_general | solution.py:34
  218.9 5.3 %copy.6 = f32[512,2048]{1,0:T(8,128)} copy(f32[512,2048]{0,1:T(8,128)} %fusion.8) | data formatting | bytes 8388608
  (2 shorter events, 0.0 us)
Async XLA Ops:
  7.2 29.9 %all-gather.2.cloned.1.call-start = ((), (), s32[]{:S(2)}) async-start(), calls=%async_computation | async-start | bytes 1179648 | tf_op jit(solution)/shard_map/all_gather | solution.py:29
  7.9 199.2 %all-reduce.4.cloned.1.call-start = ((), (), s32[]{:S(2)}) async-start(), calls=%async_computation.1 | async-start | bytes 8388608 | tf_op jit(solution)/shard_map/psum | solution.py:11
  8.0 32.6 %copy-start.2 = (f32[64]{0:T(128)S(1)}, f32[64]{0:T(128)}, u32[]{:S(2)}) copy-start(f32[64]{0:T(128)} %param.4) | copy-start | bytes 772
  8.0 33.2 %copy-start.1 = (f32[64,512]{1,0:T(8,128)S(1)}, f32[64,512]{1,0:T(8,128)}, u32[]{:S(2)}) copy-start(f32[64,512]{1,0:T(8,128)} %param.3) | copy-start | bytes 393220
  54.8 152.3 %copy-start = (f32[512,512]{1,0:T(8,128)S(1)}, f32[512,512]{1,0:T(8,128)}, u32[]{:S(2)}) copy-start(f32[512,512]{1,0:T(8,128)} %all-gather.2.cloned.1.call-done) | copy-start | bytes 3145732
Sparse Core Ops, SparseCore 0:
  9.9 27.1 all-gather.1
  41.1 165.9 all-reduce.3
where the time goes:
time: 231 us
  waiting for transfers between devices  177 us (77%)
  between operations  14.8 us (6%)
  blocking collectives  12.8 us (6%)
  matrix products  12 us (5%)
  local copies, waits for them, and re-layouts  10.8 us (5%)
  other arithmetic  4.07 us (2%)
    psum x1, waiting for transfers between devices, broadcast(): return lax.psum(jnp.where(mine, shard, jnp.zeros_like(shard)), axis)  147 us
    all_gather x1, waiting for transfers between devices, per_device(): column_panel = lax.all_gather(jacobian, 'col', axis=0, tiled=True)  29.1 us
    psum x1, blocking collectives, per_device(): lax.psum((partial_value, jnp.sum(residual * residual)), 'col')  12.8 us
    dot_general x1, matrix products, per_device(): lax.dot_general(column_panel, partner_cols, (((0,), (0,)), ((), ())), pre...  11.8 us
    unnamed x8, local copies, waits for them, and re-layouts  10.8 us
  transfers between devices with their start and end apart: 2, of which 2 were waited for; matrix products, arithmetic and copies ran while one was open for 3% of the time, Pallas kernels for 0%

commit v1 on v0

v1 whole, which is shorter than its diff:
```python
import functools

import jax
import jax.numpy as jnp
from jax import lax
from jax.experimental import pallas as pl
from jax.experimental.pallas import tpu as pltpu
from jax.sharding import PartitionSpec as P

damping_scale = 0.2
Z, Y, X, K = 8, 4, 4, 2
BLOCK = 512
ROWS = 64
PACK = ROWS + 8
VMEM = 16 * 1024 * 1024

SHIFT = (0, 4, 1, 7, 2, 6, 3, 5)
ALONG = (0, 2, 6, 1, 3, 7, 5, 4)


def place(z, y, x, k):
    return ((z % Z) * Y + y % Y) * X * K + (x % X) * K + k


def permute(array, where):
    pairs = [
        (place(z, y, x, k), place(*where(z, y, x, k)))
        for z in range(Z)
        for y in range(Y)
        for x in range(X)
        for k in range(K)
    ]
    return lax.ppermute(array, ("row", "col"), pairs)


def fetch(array, z=0, y=0):
    return permute(array, lambda z0, y0, x, k: (z0 - z, y0 - y, x, k))


def swap(array, x=0, k=0):
    return permute(array, lambda z, y, x0, k0: (z, y, x0 ^ x, k0 ^ k))


def spread(array):
    return permute(array, lambda z, y, x, k: (z + SHIFT[x * K + k], y, z // K, z % K))


def join(*arrays):
    return jnp.concatenate(arrays, axis=0)


def block_of(shift):
    return jnp.where(shift < 4, 2 * shift, (2 * (Z - shift) + 1) % Z)


def split(array):
    top = array.astype(jnp.bfloat16)
    return top, (array - top.astype(jnp.float32)).astype(jnp.bfloat16)


def panel_kernel(where, panel, high, low, gradient, damping, ordered):
    col_index = where[1]
    total = jnp.zeros((8, BLOCK), jnp.float32)
    squares = jnp.zeros((8, ROWS), jnp.float32)
    for d, along in enumerate(ALONG):
        block = block_of((where[2] + (along + Z) - col_index) % Z)
        apart = block ^ col_index
        start = pl.multiple_of((apart // K + X * (apart % K)) * PACK, 8)
        rows = panel[pl.ds(start, ROWS), :]
        residual = panel[pl.ds(start + ROWS, 8), :][:, :ROWS]
        squares += residual * residual
        total += lax.dot_general(
            residual,
            rows,
            (((1,), (0,)), ((), ())),
            precision=lax.Precision.HIGHEST,
            preferred_element_type=jnp.float32,
        )
        ordered[d * ROWS : (d + 1) * ROWS, :] = rows
    gradient[...] = jnp.sum(total, axis=0, keepdims=True)
    mean = jnp.sum(squares, keepdims=True) / (ROWS * X * K)
    damping[...] = jnp.broadcast_to(damping_scale * jnp.sqrt(mean + 1e-06), damping.shape)
    high[...], low[...] = split(ordered[...].T)


def times(a, b):
    return lax.dot_general(
        a, b, (((1,), (0,)), ((), ())), preferred_element_type=jnp.float32
    )


def cross_kernel(where, *refs, counts, diagonal):
    pieces = refs[: sum(counts)]
    high, low, damping, prior = refs[sum(counts) :][:4]
    out, top, rest = refs[-3:]
    step = pl.program_id(0)
    first = 0
    for i, count in enumerate(counts):
        mine = pieces[first : first + count]
        first += count

        @pl.when(step == i)
        def _():
            at = 0
            for piece in mine:
                end = at + piece.shape[0]
                top[at:end, :], rest[at:end, :] = split(piece[...])
                at = end

    cross = times(high[...], top[...])
    cross += times(high[...], rest[...]) + times(low[...], top[...])
    if diagonal:
        row = lax.broadcasted_iota(jnp.int32, cross.shape, 0)
        col = lax.broadcasted_iota(jnp.int32, cross.shape, 1)
        marked = (row == col) & (step == 0) & (where[1] == where[2])
        cross = cross * jnp.where(marked, 1.0 + damping[0:1, 0:1], 1.0)
    out[...] = prior[...] + cross


def full(shape):
    return pl.BlockSpec(shape, lambda i, w: (0, 0))


def kernel(body, grid, in_specs, out_specs, out_shape, name, scratch=(), aliases=None):
    return pl.pallas_call(
        body,
        grid_spec=pltpu.PrefetchScalarGridSpec(
            num_scalar_prefetch=1,
            grid=grid,
            in_specs=in_specs,
            out_specs=out_specs,
            scratch_shapes=scratch,
        ),
        out_shape=out_shape,
        input_output_aliases=aliases or {},
        compiler_params=pltpu.CompilerParams(vmem_limit_bytes=VMEM),
        cost_estimate=pl.CostEstimate(flops=1000, bytes_accessed=1000, transcendentals=0),
        name=name,
    )


def per_device(jacobian, residual, normal_prior):
    row_index, col_index = lax.axis_index("row"), lax.axis_index("col")
    where = jnp.stack([row_index % Y, col_index, row_index // Y]).astype(jnp.int32)

    together = lax.optimization_barrier
    shard = spread(jacobian)
    tail = jnp.zeros((8, BLOCK), jnp.float32).at[0, :ROWS].set(residual)
    own = join(jacobian, tail)
    own = join(own, swap(own, x=1))

    up, down = fetch(shard, z=2), fetch(shard, z=-2)
    far = fetch(shard, y=2)
    own = join(own, swap(own, x=2))
    up, down, far = together((up, down, far))
    ups, downs = fetch(join(shard, up), z=1), fetch(join(shard, down), z=-1)
    across = fetch(up, z=2)
    up_far, down_far = fetch(far, z=2), fetch(far, z=-2)
    own = join(own, swap(own, k=1))
    column = [join(shard, up, down), join(ups, downs, across)]
    column_near = [fetch(part, y=1) for part in column]
    column_back = [fetch(part, y=3) for part in column]
    ups_far, downs_far = fetch(join(far, up_far), z=1), fetch(join(far, down_far), z=-1)
    across_far = fetch(down_far, z=-2)
    column_far = [far, up_far, down_far, ups_far, downs_far, across_far]

    half = jax.ShapeDtypeStruct((BLOCK, BLOCK), jnp.bfloat16)
    outs = [half, half, jax.ShapeDtypeStruct((1, BLOCK), jnp.float32)]
    outs += [jax.ShapeDtypeStruct((8, 128), jnp.float32)]
    high, low, gradient, damping = kernel(
        panel_kernel,
        (1,),
        [full(own.shape)],
        [full(s.shape) for s in outs],
        outs,
        "own_panel",
        [pltpu.VMEM((BLOCK, BLOCK), jnp.float32)],
    )(where, own)

    def cross(columns, first, before=()):
        block = pl.BlockSpec((BLOCK, BLOCK), lambda i, w: (0, (2 * i + first + w[0]) % Y))
        pieces = [piece for column in columns for piece in column]
        counts = tuple(len(column) for column in columns)
        return kernel(
            functools.partial(cross_kernel, counts=counts, diagonal=first == 0),
            (len(columns),),
            [full(piece.shape) for piece in pieces]
            + [full(high.shape)] * 2
            + [full(damping.shape), block]
            + [pl.BlockSpec(memory_space=pl.ANY)] * len(before),
            block,
            jax.ShapeDtypeStruct(normal_prior.shape, jnp.float32),
            f"cross_{first}",
            [pltpu.VMEM((BLOCK, BLOCK), jnp.bfloat16)] * 2,
            {len(pieces) + 5: 0} if before else None,
        )(where, *pieces, high, low, damping, normal_prior, *before)

    normal = cross([column, column_far], 0)
    normal = cross([column_near, column_back], 1, (normal,))
    return normal, gradient.reshape(BLOCK)


def solution(mesh):
    return jax.shard_map(
        per_device,
        mesh=mesh,
        in_specs=(P("col", "row"), P("col"), P("row", "col")),
        out_specs=(P("row", "col"), P("row")),
        check_vma=False,
    )
```

time: 231 us -> 81.7 us (0.35)
  waiting for transfers between devices: 177 us -> 25.1 us
  starting transfers between devices: 0.08 us -> 41.5 us
  between operations: 14.8 us -> 0.75 us
  blocking collectives: 12.8 us -> 0 us
  matrix products: 12 us -> 0 us
  Pallas kernels: 0 us -> 9.85 us
  local copies, waits for them, and re-layouts: 10.8 us -> 1.74 us
    psum x1 -> x0, waiting for transfers between devices: 147 us -> none  [broadcast(): return lax.psum(jnp.where(mine, shard, jnp.zeros_like(shard)), axis)]
    ppermute x0 -> x19, starting transfers between devices: none -> 41.5 us  [permute(): return lax.ppermute(array, ('row', 'col'), pairs)]
    all_gather x1 -> x0, waiting for transfers between devices: 29.1 us -> none  [per_device(): column_panel = lax.all_gather(jacobian, 'col', axis=0, tiled=True)]
    ppermute x0 -> x19, waiting for transfers between devices: none -> 25.1 us  [permute(): return lax.ppermute(array, ('row', 'col'), pairs)]
    psum x1 -> x0, blocking collectives: 12.8 us -> none  [per_device(): lax.psum((partial_value, jnp.sum(residual * residual)), 'col')]
    dot_general x2 -> x0, matrix products: 12 us -> none  [the longest x1 11.8 us: per_device(): lax.dot_general(column_panel, partner_cols, (((0,), (0,)), ((), ())), pre...]
    pallas_call x0 -> x3, Pallas kernels: none -> 9.85 us  [the longest x2 8.13 us: cross(): kernel(functools.partial(cross_kernel, counts=counts, diagonal=first == 0...]
    unnamed x8 -> x11, local copies, waits for them, and re-layouts: 10.8 us -> 1.01 us
  transfers between devices with their start and end apart: 2 -> 19, of which waited for: 2 -> 9; matrix products, arithmetic and copies ran while one was open for 3% -> 2% of each run, Pallas kernels for 0% -> 7%
where the time goes in v1:
time: 81.7 us; the launch traced here: 81 us
  starting transfers between devices  41.5 us (51%)
  waiting for transfers between devices  25.1 us (31%)
  Pallas kernels  9.85 us (12%)
  other arithmetic  2.05 us (3%)
  local copies, waits for them, and re-layouts  1.74 us (2%)
    ppermute x19, starting transfers between devices, permute(): return lax.ppermute(array, ('row', 'col'), pairs)  41.5 us
    ppermute x19, waiting for transfers between devices, permute(): return lax.ppermute(array, ('row', 'col'), pairs)  25.1 us
    pallas_call x2, Pallas kernels, cross(): kernel(functools.partial(cross_kernel, counts=counts, diagonal=first == 0...  8.13 us
    concatenate x5, other arithmetic, join(): return jnp.concatenate(arrays, axis=0)  1.97 us
    pallas_call x1, Pallas kernels, per_device(): kernel(panel_kernel, (1,), [full(own.shape)], [full(s.shape) for s in out...  1.72 us
  transfers between devices with their start and end apart: 19, of which 9 were waited for; matrix products, arithmetic and copies ran while one was open for 2% of the time, Pallas kernels for 7%

profile of v1, /device:TPU:2, one launch (start us, length us, event | category | flops | bytes accessed | tf_op | source)
XLA Modules:
  0.0 81.0 jit_solution(17462137160269476561)
XLA Ops:
  0.6 0.9 %constant_dynamic-update-slice_fusion.10 = f32[576,512]{1,0:T(8,128)S(1)} fusion(f32[64,512]{1,0:T(8,128)} %param.5), kind=kLoop, calls=%fused_computation.17 | loop fusion | bytes 262144
  1.5 0.7 fusion
  2.2 0.9 %pad_maximum_fusion.6 = f32[72,512]{1,0:T(8,128)S(1)} fusion(f32[8,512]{1,0:T(8,128)S(1)} %get-tuple-element.32, f32[64,512]{1,0:T(8,128)} %param.5), kind=kLoop, calls=%fused_computation.6 | loop fusion | flops 36864 | bytes 294912 | tf_op jit(solution)/shard_map/concatenate | solution.py:49
  3.1 2.4 %collective-permute-start.11 = (f32[72,512]{1,0:T(8,128)S(1)}, f32[72,512]{1,0:T(8,128)S(1)}, u32[]{:S(2)}, u32[]{:S(2)}) collective-permute-start(f32[72,512]{1,0:T(8,128)S(1)} %pad_maximum_fusion.6), channel_id=1, source_target_pairs={{0,2},{1,3},{2,0},{3,1},{4,6},{5,7},{6,4},{7,5},{8,10},{9,11},{10,... | collective-permute-start | bytes 442376 | tf_op jit(solution)/shard_map/ppermute | solution.py:33
  5.5 3.0 %collective-permute-start = (f32[64,512]{1,0:T(8,128)}, f32[64,512]{1,0:T(8,128)S(1)}, u32[]{:S(2)}, u32[]{:S(2)}) collective-permute-start(f32[64,512]{1,0:T(8,128)} %param.5), channel_id=1, source_target_pairs={{0,0},{1,128},{2,32},{3,224},{4,64},{5,192},{6,96},{7,160},{8,8},{... | collective-permute-start | bytes 393224 | tf_op jit(solution)/shard_map/ppermute | solution.py:33
  8.5 6.9 %collective-permute-done = f32[64,512]{1,0:T(8,128)S(1)} collective-permute-done((f32[64,512]{1,0:T(8,128)}, f32[64,512]{1,0:T(8,128)S(1)}, u32[]{:S(2)}, u32[]{:S(2)}) %collective-permute-start) | collective-permute-done | bytes 131104 | tf_op jit(solution)/shard_map/ppermute | solution.py:33
  15.4 0.3 collective-permute-start.3
  15.7 1.5 %collective-permute-start.2 = (f32[64,512]{1,0:T(8,128)S(1)}, f32[64,512]{1,0:T(8,128)S(1)}, u32[]{:S(2)}, u32[]{:S(2)}) collective-permute-start(f32[64,512]{1,0:T(8,128)S(1)} %collective-permute-done), channel_id=1, source_target_pairs={{0,64},{1,65},{2,66},{3,67},{4,68},{5,69},{6,70},{7,71},{8,72},{9,... | collective-permute-start | bytes 393224 | tf_op jit(solution)/shard_map/ppermute | solution.py:33
  17.3 8.7 %collective-permute-start.1 = (f32[64,512]{1,0:T(8,128)S(1)}, f32[64,512]{1,0:T(8,128)S(1)}, u32[]{:S(2)}, u32[]{:S(2)}) collective-permute-start(f32[64,512]{1,0:T(8,128)S(1)} %collective-permute-done), channel_id=1, source_target_pairs={{0,192},{1,193},{2,194},{3,195},{4,196},{5,197},{6,198},{7,199},{8... | collective-permute-start | bytes 393224 | tf_op jit(solution)/shard_map/ppermute | solution.py:33
  25.9 0.0 collective-permute-done.11
  25.9 0.9 %pad_maximum_fusion.5 = f32[144,512]{1,0:T(8,128)S(1)} fusion(f32[72,512]{1,0:T(8,128)S(1)} %collective-permute-done.11, f32[8,512]{1,0:T(8,128)S(1)} %get-tuple-element.32, f32[64,512]{1,0:T(8,128)} %param.5), kind=kLoop, calls=%fused_computation.5 | loop fusion | flops 147456 | bytes 589824 | tf_op jit(solution)/shard_map/concatenate | solution.py:49
  26.9 0.0 copy-start.1
  26.9 1.1 %collective-permute-start.12 = (f32[144,512]{1,0:T(8,128)S(1)}, f32[144,512]{1,0:T(8,128)S(1)}, u32[]{:S(2)}, u32[]{:S(2)}) collective-permute-start(f32[144,512]{1,0:T(8,128)S(1)} %pad_maximum_fusion.5), channel_id=1, source_target_pairs={{0,4},{1,5},{2,6},{3,7},{4,0},{5,1},{6,2},{7,3},{8,12},{9,13},{10,... | collective-permute-start | bytes 884744 | tf_op jit(solution)/shard_map/ppermute | solution.py:33
  28.0 0.0 collective-permute-done.3.refs_2_
  28.0 2.2 %collective-permute-done.2 = f32[64,512]{1,0:T(8,128)S(1)} collective-permute-done((f32[64,512]{1,0:T(8,128)S(1)}, f32[64,512]{1,0:T(8,128)S(1)}, u32[]{:S(2)}, u32[]{:S(2)}) %collective-permute-start.2) | collective-permute-done | bytes 131104 | tf_op jit(solution)/shard_map/ppermute | solution.py:33
  30.1 1.0 %collective-permute-done.1 = f32[64,512]{1,0:T(8,128)S(1)} collective-permute-done((f32[64,512]{1,0:T(8,128)S(1)}, f32[64,512]{1,0:T(8,128)S(1)}, u32[]{:S(2)}, u32[]{:S(2)}) %collective-permute-start.1) | collective-permute-done | bytes 131104 | tf_op jit(solution)/shard_map/ppermute | solution.py:33
  31.1 2.1 %collective-permute-start.15 = (f32[64,512]{1,0:T(8,128)S(1)}, f32[64,512]{1,0:T(8,128)S(1)}, u32[]{:S(2)}, u32[]{:S(2)}) collective-permute-start(f32[64,512]{1,0:T(8,128)S(1)} %collective-permute-done.3.refs_2_), channel_id=1, source_target_pairs={{0,64},{1,65},{2,66},{3,67},{4,68},{5,69},{6,70},{7,71},{8,72},{9,... | collective-permute-start | bytes 393224 | tf_op jit(solution)/shard_map/ppermute | solution.py:33
  33.2 2.5 %collective-permute-start.14 = (f32[64,512]{1,0:T(8,128)S(1)}, f32[64,512]{1,0:T(8,128)S(1)}, u32[]{:S(2)}, u32[]{:S(2)}) collective-permute-start(f32[64,512]{1,0:T(8,128)S(1)} %collective-permute-done.3.refs_2_), channel_id=1, source_target_pairs={{0,192},{1,193},{2,194},{3,195},{4,196},{5,197},{6,198},{7,199},{8... | collective-permute-start | bytes 393224 | tf_op jit(solution)/shard_map/ppermute | solution.py:33
  35.7 1.6 %collective-permute-start.5 = (f32[128,512]{1,0:T(8,128)S(1)}, f32[128,512]{1,0:T(8,128)S(1)}, u32[]{:S(2)}, u32[]{:S(2)}) collective-permute-start(f32[128,512]{1,0:T(8,128)S(1)} %get-tuple-element.31), channel_id=1, source_target_pairs={{0,224},{1,225},{2,226},{3,227},{4,228},{5,229},{6,230},{7,231},{8... | collective-permute-start | bytes 786440 | tf_op jit(solution)/shard_map/ppermute | solution.py:33
  37.4 4.2 %collective-permute-start.7 = (f32[64,512]{1,0:T(8,128)S(1)}, f32[64,512]{1,0:T(8,128)S(1)}, u32[]{:S(2)}, u32[]{:S(2)}) collective-permute-start(f32[64,512]{1,0:T(8,128)S(1)} %collective-permute-done.1), channel_id=1, source_target_pairs={{0,192},{1,193},{2,194},{3,195},{4,196},{5,197},{6,198},{7,199},{8... | collective-permute-start | bytes 393224 | tf_op jit(solution)/shard_map/ppermute | solution.py:33
  41.6 0.0 collective-permute-done.15.refs_4_
  41.6 1.4 %collective-permute-start.6 = (f32[128,512]{1,0:T(8,128)S(1)}, f32[128,512]{1,0:T(8,128)S(1)}, u32[]{:S(2)}, u32[]{:S(2)}) collective-permute-start(f32[128,512]{1,0:T(8,128)S(1)} %get-tuple-element.30), channel_id=1, source_target_pairs={{0,32},{1,33},{2,34},{3,35},{4,36},{5,37},{6,38},{7,39},{8,40},{9,... | collective-permute-start | bytes 786440 | tf_op jit(solution)/shard_map/ppermute | solution.py:33
  43.0 0.0 collective-permute-done.14.refs_3_
  43.1 4.4 %collective-permute-start.17 = (f32[128,512]{1,0:T(8,128)S(1)}, f32[128,512]{1,0:T(8,128)S(1)}, u32[]{:S(2)}, u32[]{:S(2)}) collective-permute-start(f32[128,512]{1,0:T(8,128)S(1)} %get-tuple-element.28), channel_id=1, source_target_pairs={{0,32},{1,33},{2,34},{3,35},{4,36},{5,37},{6,38},{7,39},{8,40},{9,... | collective-permute-start | bytes 786440 | tf_op jit(solution)/shard_map/ppermute | solution.py:33
  47.5 0.0 collective-permute-done.12
  47.5 0.8 collective-permute-start.18
  48.3 0.0 copy-done.1
  48.3 1.6 %collective-permute-done.5 = f32[128,512]{1,0:T(8,128)S(1)} collective-permute-done((f32[128,512]{1,0:T(8,128)S(1)}, f32[128,512]{1,0:T(8,128)S(1)}, u32[]{:S(2)}, u32[]{:S(2)}) %collective-permute-start.5) | collective-permute-done | bytes 262176 | tf_op jit(solution)/shard_map/ppermute | solution.py:33
  49.9 0.0 collective-permute-start.13
  50.0 2.4 %collective-permute-done.6 = f32[128,512]{1,0:T(8,128)S(1)} collective-permute-done((f32[128,512]{1,0:T(8,128)S(1)}, f32[128,512]{1,0:T(8,128)S(1)}, u32[]{:S(2)}, u32[]{:S(2)}) %collective-permute-start.6) | collective-permute-done | bytes 262176 | tf_op jit(solution)/shard_map/ppermute | solution.py:33
  52.4 0.4 collective-permute-done.7
  52.8 0.8 collective-permute-start.10
  53.5 2.6 %collective-permute-start.8 = (f32[320,512]{1,0:T(8,128)S(1)}, f32[320,512]{1,0:T(8,128)S(1)}, u32[]{:S(2)}, u32[]{:S(2)}) collective-permute-start(f32[320,512]{1,0:T(8,128)S(1)} %constant_dynamic-update-slice_fusion.3.refs_1_), channel_id=1, source_target_pairs={{0,24},{1,25},{2,26},{3,27},{4,28},{5,29},{6,30},{7,31},{8,0},{9,1... | collective-permute-start | bytes 1966088 | tf_op jit(solution)/shard_map/ppermute | solution.py:33
  56.1 3.4 %collective-permute-done.18.refs_7_ = f32[64,512]{1,0:T(8,128)S(1)} collective-permute-done((f32[64,512]{1,0:T(8,128)S(1)}, f32[64,512]{1,0:T(8,128)S(1)}, u32[]{:S(2)}, u32[]{:S(2)}) %collective-permute-start.18) | collective-permute-done | bytes 131104 | tf_op jit(solution)/shard_map/ppermute | solution.py:33
  59.5 0.7 collective-permute-start.9
  60.2 0.0 collective-permute-done.17.refs_6_
  60.2 2.5 %collective-permute-start.4 = (f32[192,512]{1,0:T(8,128)S(1)}, f32[192,512]{1,0:T(8,128)S(1)}, u32[]{:S(2)}, u32[]{:S(2)}) collective-permute-start(f32[192,512]{1,0:T(8,128)S(1)} %constant_dynamic-update-slice_fusion.refs_0_), channel_id=1, source_target_pairs={{0,24},{1,25},{2,26},{3,27},{4,28},{5,29},{6,30},{7,31},{8,0},{9,1... | collective-permute-start | bytes 1179656 | tf_op jit(solution)/shard_map/ppermute | solution.py:33
  62.8 0.1 pad_add_fusion.where
  62.8 0.0 collective-permute-done.13
  62.8 1.0 %collective-permute-start.16 = (f32[128,512]{1,0:T(8,128)S(1)}, f32[128,512]{1,0:T(8,128)S(1)}, u32[]{:S(2)}, u32[]{:S(2)}) collective-permute-start(f32[128,512]{1,0:T(8,128)S(1)} %get-tuple-element.29), channel_id=1, source_target_pairs={{0,224},{1,225},{2,226},{3,227},{4,228},{5,229},{6,230},{7,231},{8... | collective-permute-start | bytes 786440 | tf_op jit(solution)/shard_map/ppermute | solution.py:33
  63.9 1.7 %own_panel.1 = (bf16[512,512]{1,0:T(8,128)(2,1)S(1)}, bf16[512,512]{1,0:T(8,128)(2,1)S(1)}, f32[1,512]{1,0:T(1,128)}, f32[8,128]{1,0:T(8,128)S(1)}) custom-call(s32[3]{0:T(128)S(1)} %pad_add_fusion.where, f32[576,512]{1,0:T(8,128)S(1)} %constant_dynamic-update-slice_fusion.6.panel), custom_call_target="tpu_custom_call" | custom-call | flops 1000 | bytes 1000 | tf_op jit(solution)/shard_map/own_panel/pallas_call | solution.py:170
  65.6 4.5 %collective-permute-done.16.refs_5_ = f32[128,512]{1,0:T(8,128)S(1)} collective-permute-done((f32[128,512]{1,0:T(8,128)S(1)}, f32[128,512]{1,0:T(8,128)S(1)}, u32[]{:S(2)}, u32[]{:S(2)}) %collective-permute-start.16) | collective-permute-done | bytes 262176 | tf_op jit(solution)/shard_map/ppermute | solution.py:33
  70.1 4.0 %cross_0.1.refs_8_ = f32[512,2048]{1,0:T(8,128)} custom-call(s32[3]{0:T(128)S(1)} %pad_add_fusion.where, f32[192,512]{1,0:T(8,128)S(1)} %constant_dynamic-update-slice_fusion.refs_0_, f32[320,512]{1,0:T(8,128)S(1)} %constant_dynamic-update-slice_fusion.3.refs_1_, f32[64,512]{1,0:T(8,128)S(1)} %collective-permute-done.3.refs_2_, ...), custom_call_target="tpu_custom_call" | custom-call | flops 1000 | bytes 1000 | tf_op jit(solution)/shard_map/cross_0/pallas_call | solution.py:184
  74.1 2.8 %collective-permute-done.9.refs_2_ = f32[192,512]{1,0:T(8,128)S(1)} collective-permute-done((f32[192,512]{1,0:T(8,128)S(1)}, f32[192,512]{1,0:T(8,128)S(1)}, u32[]{:S(2)}, u32[]{:S(2)}) %collective-permute-start.9) | collective-permute-done | bytes 393248 | tf_op jit(solution)/shard_map/ppermute | solution.py:33
  76.9 0.0 collective-permute-done.4.refs_0_
  76.9 0.0 collective-permute-done.10.refs_3_
  76.9 0.0 collective-permute-done.8.refs_1_
  76.9 4.1 %cross_1.1 = f32[512,2048]{1,0:T(8,128)} custom-call(s32[3]{0:T(128)S(1)} %pad_add_fusion.where, f32[192,512]{1,0:T(8,128)S(1)} %collective-permute-done.4.refs_0_, f32[320,512]{1,0:T(8,128)S(1)} %collective-permute-done.8.refs_1_, f32[192,512]{1,0:T(8,128)S(1)} %collective-permute-done.9.refs_2_, ...), custom_call_target="tpu_custom_call", output_to_operand_aliasing={{}: (9, {})} | custom-call | flops 1000 | bytes 1000 | tf_op jit(solution)/shard_map/cross_1/pallas_call | solution.py:184
  (14 shorter events, 0.3 us)
Async XLA Ops:
  3.1 22.8 %collective-permute-start.11 = (f32[72,512]{1,0:T(8,128)S(1)}, f32[72,512]{1,0:T(8,128)S(1)}, u32[]{:S(2)}, u32[]{:S(2)}) collective-permute-start(f32[72,512]{1,0:T(8,128)S(1)} %pad_maximum_fusion.6), channel_id=1, source_target_pairs={{0,2},{1,3},{2,0},{3,1},{4,6},{5,7},{6,4},{7,5},{8,10},{9,11},{10,... | collective-permute-start | bytes 442376 | tf_op jit(solution)/shard_map/ppermute | solution.py:33
  5.5 9.9 %collective-permute-start = (f32[64,512]{1,0:T(8,128)}, f32[64,512]{1,0:T(8,128)S(1)}, u32[]{:S(2)}, u32[]{:S(2)}) collective-permute-start(f32[64,512]{1,0:T(8,128)} %param.5), channel_id=1, source_target_pairs={{0,0},{1,128},{2,32},{3,224},{4,64},{5,192},{6,96},{7,160},{8,8},{... | collective-permute-start | bytes 393224 | tf_op jit(solution)/shard_map/ppermute | solution.py:33
  15.4 12.6 %collective-permute-start.3 = (f32[64,512]{1,0:T(8,128)S(1)}, f32[64,512]{1,0:T(8,128)S(1)}, u32[]{:S(2)}, u32[]{:S(2)}) collective-permute-start(f32[64,512]{1,0:T(8,128)S(1)} %collective-permute-done), channel_id=1, source_target_pairs={{0,16},{1,17},{2,18},{3,19},{4,20},{5,21},{6,22},{7,23},{8,24},{9,... | collective-permute-start | bytes 393224 | tf_op jit(solution)/shard_map/ppermute | solution.py:33
  15.7 14.4 %collective-permute-start.2 = (f32[64,512]{1,0:T(8,128)S(1)}, f32[64,512]{1,0:T(8,128)S(1)}, u32[]{:S(2)}, u32[]{:S(2)}) collective-permute-start(f32[64,512]{1,0:T(8,128)S(1)} %collective-permute-done), channel_id=1, source_target_pairs={{0,64},{1,65},{2,66},{3,67},{4,68},{5,69},{6,70},{7,71},{8,72},{9,... | collective-permute-start | bytes 393224 | tf_op jit(solution)/shard_map/ppermute | solution.py:33
  17.3 13.8 %collective-permute-start.1 = (f32[64,512]{1,0:T(8,128)S(1)}, f32[64,512]{1,0:T(8,128)S(1)}, u32[]{:S(2)}, u32[]{:S(2)}) collective-permute-start(f32[64,512]{1,0:T(8,128)S(1)} %collective-permute-done), channel_id=1, source_target_pairs={{0,192},{1,193},{2,194},{3,195},{4,196},{5,197},{6,198},{7,199},{8... | collective-permute-start | bytes 393224 | tf_op jit(solution)/shard_map/ppermute | solution.py:33
  26.9 21.4 %copy-start.1 = (f32[64,512]{1,0:T(8,128)S(1)}, f32[64,512]{1,0:T(8,128)}, u32[]{:S(2)}) copy-start(f32[64,512]{1,0:T(8,128)} %param.5) | copy-start | bytes 393220
  26.9 20.6 %collective-permute-start.12 = (f32[144,512]{1,0:T(8,128)S(1)}, f32[144,512]{1,0:T(8,128)S(1)}, u32[]{:S(2)}, u32[]{:S(2)}) collective-permute-start(f32[144,512]{1,0:T(8,128)S(1)} %pad_maximum_fusion.5), channel_id=1, source_target_pairs={{0,4},{1,5},{2,6},{3,7},{4,0},{5,1},{6,2},{7,3},{8,12},{9,13},{10,... | collective-permute-start | bytes 884744 | tf_op jit(solution)/shard_map/ppermute | solution.py:33
  31.1 10.5 %collective-permute-start.15 = (f32[64,512]{1,0:T(8,128)S(1)}, f32[64,512]{1,0:T(8,128)S(1)}, u32[]{:S(2)}, u32[]{:S(2)}) collective-permute-start(f32[64,512]{1,0:T(8,128)S(1)} %collective-permute-done.3.refs_2_), channel_id=1, source_target_pairs={{0,64},{1,65},{2,66},{3,67},{4,68},{5,69},{6,70},{7,71},{8,72},{9,... | collective-permute-start | bytes 393224 | tf_op jit(solution)/shard_map/ppermute | solution.py:33
  33.2 9.8 %collective-permute-start.14 = (f32[64,512]{1,0:T(8,128)S(1)}, f32[64,512]{1,0:T(8,128)S(1)}, u32[]{:S(2)}, u32[]{:S(2)}) collective-permute-start(f32[64,512]{1,0:T(8,128)S(1)} %collective-permute-done.3.refs_2_), channel_id=1, source_target_pairs={{0,192},{1,193},{2,194},{3,195},{4,196},{5,197},{6,198},{7,199},{8... | collective-permute-start | bytes 393224 | tf_op jit(solution)/shard_map/ppermute | solution.py:33
  35.7 14.2 %collective-permute-start.5 = (f32[128,512]{1,0:T(8,128)S(1)}, f32[128,512]{1,0:T(8,128)S(1)}, u32[]{:S(2)}, u32[]{:S(2)}) collective-permute-start(f32[128,512]{1,0:T(8,128)S(1)} %get-tuple-element.31), channel_id=1, source_target_pairs={{0,224},{1,225},{2,226},{3,227},{4,228},{5,229},{6,230},{7,231},{8... | collective-permute-start | bytes 786440 | tf_op jit(solution)/shard_map/ppermute | solution.py:33
  37.4 15.4 %collective-permute-start.7 = (f32[64,512]{1,0:T(8,128)S(1)}, f32[64,512]{1,0:T(8,128)S(1)}, u32[]{:S(2)}, u32[]{:S(2)}) collective-permute-start(f32[64,512]{1,0:T(8,128)S(1)} %collective-permute-done.1), channel_id=1, source_target_pairs={{0,192},{1,193},{2,194},{3,195},{4,196},{5,197},{6,198},{7,199},{8... | collective-permute-start | bytes 393224 | tf_op jit(solution)/shard_map/ppermute | solution.py:33
  41.6 10.8 %collective-permute-start.6 = (f32[128,512]{1,0:T(8,128)S(1)}, f32[128,512]{1,0:T(8,128)S(1)}, u32[]{:S(2)}, u32[]{:S(2)}) collective-permute-start(f32[128,512]{1,0:T(8,128)S(1)} %get-tuple-element.30), channel_id=1, source_target_pairs={{0,32},{1,33},{2,34},{3,35},{4,36},{5,37},{6,38},{7,39},{8,40},{9,... | collective-permute-start | bytes 786440 | tf_op jit(solution)/shard_map/ppermute | solution.py:33
  43.1 17.2 %collective-permute-start.17 = (f32[128,512]{1,0:T(8,128)S(1)}, f32[128,512]{1,0:T(8,128)S(1)}, u32[]{:S(2)}, u32[]{:S(2)}) collective-permute-start(f32[128,512]{1,0:T(8,128)S(1)} %get-tuple-element.28), channel_id=1, source_target_pairs={{0,32},{1,33},{2,34},{3,35},{4,36},{5,37},{6,38},{7,39},{8,40},{9,... | collective-permute-start | bytes 786440 | tf_op jit(solution)/shard_map/ppermute | solution.py:33
  47.5 12.1 %collective-permute-start.18 = (f32[64,512]{1,0:T(8,128)S(1)}, f32[64,512]{1,0:T(8,128)S(1)}, u32[]{:S(2)}, u32[]{:S(2)}) collective-permute-start(f32[64,512]{1,0:T(8,128)S(1)} %collective-permute-done.15.refs_4_), channel_id=1, source_target_pairs={{0,64},{1,65},{2,66},{3,67},{4,68},{5,69},{6,70},{7,71},{8,72},{9,... | collective-permute-start | bytes 393224 | tf_op jit(solution)/shard_map/ppermute | solution.py:33
  49.9 12.9 %collective-permute-start.13 = (f32[288,512]{1,0:T(8,128)S(1)}, f32[288,512]{1,0:T(8,128)S(1)}, u32[]{:S(2)}, u32[]{:S(2)}) collective-permute-start(f32[288,512]{1,0:T(8,128)S(1)} %pad_maximum_fusion), channel_id=1, source_target_pairs={{0,1},{1,0},{2,3},{3,2},{4,5},{5,4},{6,7},{7,6},{8,9},{9,8},{10,11... | collective-permute-start | bytes 1769480 | tf_op jit(solution)/shard_map/ppermute | solution.py:33
  52.4 17.7 %copy-start = (f32[512,2048]{1,0:T(8,128)S(1)}, f32[512,2048]{1,0:T(8,128)}, u32[]{:S(2)}) copy-start(f32[512,2048]{1,0:T(8,128)} %refs_7_.1) | copy-start | bytes 12582916
  52.8 24.1 %collective-permute-start.10 = (f32[320,512]{1,0:T(8,128)S(1)}, f32[320,512]{1,0:T(8,128)S(1)}, u32[]{:S(2)}, u32[]{:S(2)}) collective-permute-start(f32[320,512]{1,0:T(8,128)S(1)} %constant_dynamic-update-slice_fusion.3.refs_1_), channel_id=1, source_target_pairs={{0,8},{1,9},{2,10},{3,11},{4,12},{5,13},{6,14},{7,15},{8,16},{9,17... | collective-permute-start | bytes 1966088 | tf_op jit(solution)/shard_map/ppermute | solution.py:33
  53.5 23.4 %collective-permute-start.8 = (f32[320,512]{1,0:T(8,128)S(1)}, f32[320,512]{1,0:T(8,128)S(1)}, u32[]{:S(2)}, u32[]{:S(2)}) collective-permute-start(f32[320,512]{1,0:T(8,128)S(1)} %constant_dynamic-update-slice_fusion.3.refs_1_), channel_id=1, source_target_pairs={{0,24},{1,25},{2,26},{3,27},{4,28},{5,29},{6,30},{7,31},{8,0},{9,1... | collective-permute-start | bytes 1966088 | tf_op jit(solution)/shard_map/ppermute | solution.py:33
  59.5 17.4 %collective-permute-start.9 = (f32[192,512]{1,0:T(8,128)S(1)}, f32[192,512]{1,0:T(8,128)S(1)}, u32[]{:S(2)}, u32[]{:S(2)}) collective-permute-start(f32[192,512]{1,0:T(8,128)S(1)} %constant_dynamic-update-slice_fusion.refs_0_), channel_id=1, source_target_pairs={{0,8},{1,9},{2,10},{3,11},{4,12},{5,13},{6,14},{7,15},{8,16},{9,17... | collective-permute-start | bytes 1179656 | tf_op jit(solution)/shard_map/ppermute | solution.py:33
  60.2 16.7 %collective-permute-start.4 = (f32[192,512]{1,0:T(8,128)S(1)}, f32[192,512]{1,0:T(8,128)S(1)}, u32[]{:S(2)}, u32[]{:S(2)}) collective-permute-start(f32[192,512]{1,0:T(8,128)S(1)} %constant_dynamic-update-slice_fusion.refs_0_), channel_id=1, source_target_pairs={{0,24},{1,25},{2,26},{3,27},{4,28},{5,29},{6,30},{7,31},{8,0},{9,1... | collective-permute-start | bytes 1179656 | tf_op jit(solution)/shard_map/ppermute | solution.py:33
  62.8 7.2 %collective-permute-start.16 = (f32[128,512]{1,0:T(8,128)S(1)}, f32[128,512]{1,0:T(8,128)S(1)}, u32[]{:S(2)}, u32[]{:S(2)}) collective-permute-start(f32[128,512]{1,0:T(8,128)S(1)} %get-tuple-element.29), channel_id=1, source_target_pairs={{0,224},{1,225},{2,226},{3,227},{4,228},{5,229},{6,230},{7,231},{8... | collective-permute-start | bytes 786440 | tf_op jit(solution)/shard_map/ppermute | solution.py:33

commit v2 on v1

--- a/solution.py
+++ b/solution.py
@@ -41,8 +41,8 @@
     return permute(array, lambda z, y, x0, k0: (z, y, x0 ^ x, k0 ^ k))
 
 
-def spread(array):
-    return permute(array, lambda z, y, x, k: (z + SHIFT[x * K + k], y, z // K, z % K))
+def spread(array, y=0):
+    return permute(array, lambda z, y0, x, k: (z + SHIFT[x * K + k], y0 - y, z // K, z % K))
 
 
 def join(*arrays):
@@ -58,7 +58,7 @@
     return top, (array - top.astype(jnp.float32)).astype(jnp.bfloat16)
 
 
-def panel_kernel(where, panel, high, low, gradient, damping, ordered):
+def panel_kernel(where, panel, both, gradient, damping, ordered):
     col_index = where[1]
     total = jnp.zeros((8, BLOCK), jnp.float32)
     squares = jnp.zeros((8, ROWS), jnp.float32)
@@ -80,7 +80,10 @@
     gradient[...] = jnp.sum(total, axis=0, keepdims=True)
     mean = jnp.sum(squares, keepdims=True) / (ROWS * X * K)
     damping[...] = jnp.broadcast_to(damping_scale * jnp.sqrt(mean + 1e-06), damping.shape)
-    high[...], low[...] = split(ordered[...].T)
+    high, low = split(ordered[...].T)
+    both[:, :BLOCK] = high
+    both[:, BLOCK : 2 * BLOCK] = high
+    both[:, 2 * BLOCK :] = low
 
 
 def times(a, b):
@@ -89,11 +92,12 @@
     )
 
 
-def cross_kernel(where, *refs, counts, diagonal):
+def cross_kernel(where, *refs, counts, which, diagonal):
     pieces = refs[: sum(counts)]
-    high, low, damping, prior = refs[sum(counts) :][:4]
-    out, top, rest = refs[-3:]
+    both, damping, prior = refs[sum(counts) :][:3]
+    out, column = refs[-2:]
     step = pl.program_id(0)
+    place = (which(step) + where[0]) % Y * BLOCK
     first = 0
     for i, count in enumerate(counts):
         mine = pieces[first : first + count]
@@ -104,21 +108,22 @@
             at = 0
             for piece in mine:
                 end = at + piece.shape[0]
-                top[at:end, :], rest[at:end, :] = split(piece[...])
+                high, low = split(piece[...])
+                column[at:end, :] = high
+                column[BLOCK + at : BLOCK + end, :] = low
+                column[2 * BLOCK + at : 2 * BLOCK + end, :] = high
                 at = end
 
-    cross = times(high[...], top[...])
-    cross += times(high[...], rest[...]) + times(low[...], top[...])
+    cross = times(both[...], column[...])
     if diagonal:
         row = lax.broadcasted_iota(jnp.int32, cross.shape, 0)
         col = lax.broadcasted_iota(jnp.int32, cross.shape, 1)
-        marked = (row == col) & (step == 0) & (where[1] == where[2])
+        marked = (row == col) & (where[1] == where[2])
         cross = cross * jnp.where(marked, 1.0 + damping[0:1, 0:1], 1.0)
-    out[...] = prior[...] + cross
-
-
-def full(shape):
-    return pl.BlockSpec(shape, lambda i, w: (0, 0))
+    out[...] = prior[:, pl.ds(pl.multiple_of(place, BLOCK), BLOCK)] + cross
+
+
+held = pl.BlockSpec(memory_space=pltpu.VMEM)
 
 
 def kernel(body, grid, in_specs, out_specs, out_shape, name, scratch=(), aliases=None):
@@ -144,59 +149,68 @@
     where = jnp.stack([row_index % Y, col_index, row_index // Y]).astype(jnp.int32)
 
     together = lax.optimization_barrier
-    shard = spread(jacobian)
+    shard, far = spread(jacobian), spread(jacobian, y=2)
     tail = jnp.zeros((8, BLOCK), jnp.float32).at[0, :ROWS].set(residual)
-    own = join(jacobian, tail)
+    shard, own = together((shard, join(jacobian, tail)))
+
+    up, down = fetch(shard, z=2), fetch(shard, z=-2)
     own = join(own, swap(own, x=1))
-
-    up, down = fetch(shard, z=2), fetch(shard, z=-2)
-    far = fetch(shard, y=2)
-    own = join(own, swap(own, x=2))
-    up, down, far = together((up, down, far))
+    up, down = together((up, down))
     ups, downs = fetch(join(shard, up), z=1), fetch(join(shard, down), z=-1)
     across = fetch(up, z=2)
     up_far, down_far = fetch(far, z=2), fetch(far, z=-2)
+    first = join(shard, up, down)
+    near, back = fetch(first, y=1), fetch(first, y=3)
+    up_far, down_far, near, back, ups, downs, across = together(
+        (up_far, down_far, near, back, ups, downs, across)
+    )
+    own = join(own, swap(own, x=2))
     own = join(own, swap(own, k=1))
-    column = [join(shard, up, down), join(ups, downs, across)]
-    column_near = [fetch(part, y=1) for part in column]
-    column_back = [fetch(part, y=3) for part in column]
+    rest = join(ups, downs, across)
+    near_rest, back_rest = fetch(rest, y=1), fetch(rest, y=3)
     ups_far, downs_far = fetch(join(far, up_far), z=1), fetch(join(far, down_far), z=-1)
     across_far = fetch(down_far, z=-2)
-    column_far = [far, up_far, down_far, ups_far, downs_far, across_far]
-
-    half = jax.ShapeDtypeStruct((BLOCK, BLOCK), jnp.bfloat16)
-    outs = [half, half, jax.ShapeDtypeStruct((1, BLOCK), jnp.float32)]
-    outs += [jax.ShapeDtypeStruct((8, 128), jnp.float32)]
-    high, low, gradient, damping = kernel(
+    columns = [
+        [first, rest],
+        [near, near_rest],
+        [far, up_far, down_far, ups_far, downs_far, across_far],
+        [back, back_rest],
+    ]
+
+    outs = [
+        jax.ShapeDtypeStruct((BLOCK, 3 * BLOCK), jnp.bfloat16),
+        jax.ShapeDtypeStruct((1, BLOCK), jnp.float32),
+        jax.ShapeDtypeStruct((8, 128), jnp.float32),
+    ]
+    both, gradient, damping = kernel(
         panel_kernel,
-        (1,),
-        [full(own.shape)],
-        [full(s.shape) for s in outs],
+        (),
+        [held],
+        [held] * len(outs),
         outs,
         "own_panel",
         [pltpu.VMEM((BLOCK, BLOCK), jnp.float32)],
     )(where, own)
 
-    def cross(columns, first, before=()):
-        block = pl.BlockSpec((BLOCK, BLOCK), lambda i, w: (0, (2 * i + first + w[0]) % Y))
-        pieces = [piece for column in columns for piece in column]
-        counts = tuple(len(column) for column in columns)
+    def cross(chosen, before=()):
+        which = lambda i: sum(dy * (i == at) for at, dy in enumerate(chosen))
+        block = pl.BlockSpec((BLOCK, BLOCK), lambda i, w: (0, (which(i) + w[0]) % Y))
+        pieces = [piece for dy in chosen for piece in columns[dy]]
+        counts = tuple(len(columns[dy]) for dy in chosen)
         return kernel(
-            functools.partial(cross_kernel, counts=counts, diagonal=first == 0),
-            (len(columns),),
-            [full(piece.shape) for piece in pieces]
-            + [full(high.shape)] * 2
-            + [full(damping.shape), block]
+            functools.partial(cross_kernel, counts=counts, which=which, diagonal=chosen == (0,)),
+            (len(chosen),),
+            [held] * (len(pieces) + 3)
             + [pl.BlockSpec(memory_space=pl.ANY)] * len(before),
             block,
             jax.ShapeDtypeStruct(normal_prior.shape, jnp.float32),
-            f"cross_{first}",
-            [pltpu.VMEM((BLOCK, BLOCK), jnp.bfloat16)] * 2,
-            {len(pieces) + 5: 0} if before else None,
-        )(where, *pieces, high, low, damping, normal_prior, *before)
-
-    normal = cross([column, column_far], 0)
-    normal = cross([column_near, column_back], 1, (normal,))
+            "cross_" + "_".join(map(str, chosen)),
+            [pltpu.VMEM((3 * BLOCK, BLOCK), jnp.bfloat16)],
+            {len(pieces) + 4: 0} if before else None,
+        )(where, *pieces, both, damping, normal_prior, *before)
+
+    normal = cross((0,))
+    normal = cross((1, 3, 2), (normal,))
     return normal, gradient.reshape(BLOCK)
 
 

time: 81.7 us -> 75.9 us (0.929)
  waiting for transfers between devices: 25.1 us -> 10.9 us
  starting transfers between devices: 41.5 us -> 46.6 us
  other arithmetic: 2.05 us -> 4.13 us
    ppermute x19, waiting for transfers between devices: 25.1 us -> 10.9 us  [permute(): return lax.ppermute(array, ('row', 'col'), pairs)]
    ppermute x19, starting transfers between devices: 41.5 us -> 46.6 us  [permute(): return lax.ppermute(array, ('row', 'col'), pairs)]
    concatenate x5 -> x6, other arithmetic: 1.97 us -> 4.05 us  [join(): return jnp.concatenate(arrays, axis=0)]
    unnamed x11 -> x14, local copies, waits for them, and re-layouts: 1.01 us -> 2.26 us
  transfers between devices with their start and end apart: 19 -> 19, of which waited for: 9 -> 7; matrix products, arithmetic and copies ran while one was open for 2% -> 6% of each run, Pallas kernels for 7% -> 6%
where the time goes in v2:
time: 75.9 us; the launch traced here: 75.1 us
  starting transfers between devices  46.6 us (61%)
  waiting for transfers between devices  10.9 us (14%)
  Pallas kernels  10.4 us (14%)
  other arithmetic  4.13 us (5%)
  local copies, waits for them, and re-layouts  2.28 us (3%)
  between operations  0.79 us (1%)
    ppermute x19, starting transfers between devices, permute(): return lax.ppermute(array, ('row', 'col'), pairs)  46.6 us
    ppermute x19, waiting for transfers between devices, permute(): return lax.ppermute(array, ('row', 'col'), pairs)  10.9 us
    pallas_call x2, Pallas kernels, cross(): kernel(functools.partial(cross_kernel, counts=counts, which=which, diagon...  8.64 us
    concatenate x6, other arithmetic, join(): return jnp.concatenate(arrays, axis=0)  4.05 us
    unnamed x14, local copies, waits for them, and re-layouts  2.26 us
    pallas_call x1, Pallas kernels, per_device(): kernel(panel_kernel, (), [held], [held] * len(outs), outs, 'own_panel', [...  1.72 us
  transfers between devices with their start and end apart: 19, of which 7 were waited for; matrix products, arithmetic and copies ran while one was open for 6% of the time, Pallas kernels for 6%

profile of v2, /device:TPU:2, one launch (start us, length us, event | category | flops | bytes accessed | tf_op | source)
XLA Modules:
  0.0 75.1 jit_solution(3326872878752901812)
XLA Ops:
  0.6 3.8 %collective-permute-start.3 = (f32[64,512]{1,0:T(8,128)}, f32[64,512]{1,0:T(8,128)S(1)}, u32[]{:S(2)}, u32[]{:S(2)}) collective-permute-start(f32[64,512]{1,0:T(8,128)} %param.5), channel_id=1, source_target_pairs={{0,0},{1,128},{2,32},{3,224},{4,64},{5,192},{6,96},{7,160},{8,8},{... | collective-permute-start | bytes 393224 | tf_op jit(solution)/shard_map/ppermute | solution.py:33
  4.4 2.7 %collective-permute-start = (f32[64,512]{1,0:T(8,128)}, f32[64,512]{1,0:T(8,128)S(1)}, u32[]{:S(2)}, u32[]{:S(2)}) collective-permute-start(f32[64,512]{1,0:T(8,128)} %param.5), channel_id=1, source_target_pairs={{0,16},{1,144},{2,48},{3,240},{4,80},{5,208},{6,112},{7,176},{8,24... | collective-permute-start | bytes 393224 | tf_op jit(solution)/shard_map/ppermute | solution.py:33
  7.2 0.9 %select_maximum_fusion = f32[72,512]{1,0:T(8,128)S(1)} fusion(f32[1,64]{1,0:T(1,128)} %bitcast.5, f32[64,512]{1,0:T(8,128)} %param.5), kind=kLoop, calls=%fused_computation.7 | loop fusion | flops 110592 | bytes 278784 | tf_op jit(solution)/shard_map/concatenate | solution.py:49
  8.1 0.9 %collective-permute-done.3 = f32[64,512]{1,0:T(8,128)S(1)} collective-permute-done((f32[64,512]{1,0:T(8,128)}, f32[64,512]{1,0:T(8,128)S(1)}, u32[]{:S(2)}, u32[]{:S(2)}) %collective-permute-start.3) | collective-permute-done | bytes 131104 | tf_op jit(solution)/shard_map/ppermute | solution.py:33
  9.0 5.0 %collective-permute-start.5 = (f32[64,512]{1,0:T(8,128)S(1)}, f32[64,512]{1,0:T(8,128)S(1)}, u32[]{:S(2)}, u32[]{:S(2)}) collective-permute-start(f32[64,512]{1,0:T(8,128)S(1)} %collective-permute-done.3), channel_id=1, source_target_pairs={{0,64},{1,65},{2,66},{3,67},{4,68},{5,69},{6,70},{7,71},{8,72},{9,... | collective-permute-start | bytes 393224 | tf_op jit(solution)/shard_map/ppermute | solution.py:33
  14.1 5.6 %collective-permute-start.4 = (f32[64,512]{1,0:T(8,128)S(1)}, f32[64,512]{1,0:T(8,128)S(1)}, u32[]{:S(2)}, u32[]{:S(2)}) collective-permute-start(f32[64,512]{1,0:T(8,128)S(1)} %collective-permute-done.3), channel_id=1, source_target_pairs={{0,192},{1,193},{2,194},{3,195},{4,196},{5,197},{6,198},{7,199},{8... | collective-permute-start | bytes 393224 | tf_op jit(solution)/shard_map/ppermute | solution.py:33
  19.7 0.2 collective-permute-start.16
  19.9 0.0 collective-permute-done.refs_4_
  20.0 0.1 collective-permute-start.2
  20.0 5.5 %collective-permute-start.1 = (f32[64,512]{1,0:T(8,128)S(1)}, f32[64,512]{1,0:T(8,128)S(1)}, u32[]{:S(2)}, u32[]{:S(2)}) collective-permute-start(f32[64,512]{1,0:T(8,128)S(1)} %collective-permute-done.refs_4_), channel_id=1, source_target_pairs={{0,192},{1,193},{2,194},{3,195},{4,196},{5,197},{6,198},{7,199},{8... | collective-permute-start | bytes 393224 | tf_op jit(solution)/shard_map/ppermute | solution.py:33
  25.6 0.0 collective-permute-done.5
  25.6 0.2 collective-permute-done.4
  25.7 0.2 collective-permute-done.16
  26.0 3.7 %collective-permute-start.17 = (f32[144,512]{1,0:T(8,128)S(1)}, f32[144,512]{1,0:T(8,128)S(1)}, u32[]{:S(2)}, u32[]{:S(2)}) collective-permute-start(f32[144,512]{1,0:T(8,128)S(1)} %pad_maximum_fusion.6), channel_id=1, source_target_pairs={{0,4},{1,5},{2,6},{3,7},{4,0},{5,1},{6,2},{7,3},{8,12},{9,13},{10,... | collective-permute-start | bytes 884744 | tf_op jit(solution)/shard_map/ppermute | solution.py:33
  29.7 0.1 collective-permute-start.7
  29.8 3.7 %collective-permute-start.6 = (f32[192,512]{1,0:T(8,128)S(1)}, f32[192,512]{1,0:T(8,128)S(1)}, u32[]{:S(2)}, u32[]{:S(2)}) collective-permute-start(f32[192,512]{1,0:T(8,128)S(1)} %constant_dynamic-update-slice_fusion.refs_0_), channel_id=1, source_target_pairs={{0,24},{1,25},{2,26},{3,27},{4,28},{5,29},{6,30},{7,31},{8,0},{9,1... | collective-permute-start | bytes 1179656 | tf_op jit(solution)/shard_map/ppermute | solution.py:33
  33.6 0.0 collective-permute-done.2.refs_6_
  33.6 5.5 %collective-permute-start.9 = (f32[128,512]{1,0:T(8,128)S(1)}, f32[128,512]{1,0:T(8,128)S(1)}, u32[]{:S(2)}, u32[]{:S(2)}) collective-permute-start(f32[128,512]{1,0:T(8,128)S(1)} %get-tuple-element.44), channel_id=1, source_target_pairs={{0,32},{1,33},{2,34},{3,35},{4,36},{5,37},{6,38},{7,39},{8,40},{9,... | collective-permute-start | bytes 786440 | tf_op jit(solution)/shard_map/ppermute | solution.py:33
  39.1 0.0 collective-permute-done.1.refs_5_
  39.1 0.0 collective-permute-start.8
  39.1 0.0 collective-permute-done.17
  39.1 0.0 copy-start.4
  39.1 2.5 %collective-permute-start.10 = (f32[64,512]{1,0:T(8,128)S(1)}, f32[64,512]{1,0:T(8,128)S(1)}, u32[]{:S(2)}, u32[]{:S(2)}) collective-permute-start(f32[64,512]{1,0:T(8,128)S(1)} %collective-permute-done.4), channel_id=1, source_target_pairs={{0,192},{1,193},{2,194},{3,195},{4,196},{5,197},{6,198},{7,199},{8... | collective-permute-start | bytes 393224 | tf_op jit(solution)/shard_map/ppermute | solution.py:33
  41.6 0.9 %pad_maximum_fusion.1 = f32[288,512]{1,0:T(8,128)} fusion(f32[144,512]{1,0:T(8,128)S(1)} %collective-permute-done.17, f32[72,512]{1,0:T(8,128)S(1)} %collective-permute-done.16, f32[72,512]{1,0:T(8,128)S(1)} %select_maximum_fusion), kind=kLoop, calls=%fused_computation.1 | loop fusion | flops 294912 | bytes 1179648 | tf_op jit(solution)/shard_map/concatenate | solution.py:49
  42.4 8.0 %collective-permute-done.10 = f32[64,512]{1,0:T(8,128)S(1)} collective-permute-done((f32[64,512]{1,0:T(8,128)S(1)}, f32[64,512]{1,0:T(8,128)S(1)}, u32[]{:S(2)}, u32[]{:S(2)}) %collective-permute-start.10) | collective-permute-done | bytes 131104 | tf_op jit(solution)/shard_map/ppermute | solution.py:33
  50.4 0.0 collective-permute-start.18
  50.4 0.0 collective-permute-done.9
  50.4 0.0 collective-permute-done.8
  50.4 0.0 collective-permute-done.7.refs_2_
  50.5 0.0 collective-permute-done.6.refs_0_
  50.5 0.2 collective-permute-start.12
  50.8 3.1 %collective-permute-start.11 = (f32[320,512]{1,0:T(8,128)S(1)}, f32[320,512]{1,0:T(8,128)S(1)}, u32[]{:S(2)}, u32[]{:S(2)}) collective-permute-start(f32[320,512]{1,0:T(8,128)S(1)} %constant_dynamic-update-slice_fusion.3.refs_1_), channel_id=1, source_target_pairs={{0,24},{1,25},{2,26},{3,27},{4,28},{5,29},{6,30},{7,31},{8,0},{9,1... | collective-permute-start | bytes 1966088 | tf_op jit(solution)/shard_map/ppermute | solution.py:33
  53.9 0.9 %pad_maximum_fusion.4 = (f32[128,512]{1,0:T(8,128)}, f32[128,512]{1,0:T(8,128)}) fusion(f32[64,512]{1,0:T(8,128)S(1)} %collective-permute-done.refs_4_, f32[64,512]{1,0:T(8,128)S(1)} %collective-permute-done.2.refs_6_, f32[64,512]{1,0:T(8,128)S(1)} %collective-permute-done.1.refs_5_), kind=kLoop, calls=%fused_computation.4 | loop fusion | flops 131072 | bytes 917504 | tf_op jit(solution)/shard_map/concatenate | solution.py:49
  54.7 0.0 collective-permute-start.14
  54.7 3.2 %collective-permute-start.13 = (f32[128,512]{1,0:T(8,128)}, f32[128,512]{1,0:T(8,128)}, u32[]{:S(2)}, u32[]{:S(2)}) collective-permute-start(f32[128,512]{1,0:T(8,128)} %get-tuple-element.43), channel_id=1, source_target_pairs={{0,224},{1,225},{2,226},{3,227},{4,228},{5,229},{6,230},{7,231},{8... | collective-permute-start | bytes 786440 | tf_op jit(solution)/shard_map/ppermute | solution.py:33
  58.0 0.1 pad_add_fusion.where
  58.1 0.0 collective-permute-done.18
  58.1 1.6 %collective-permute-start.15 = (f32[64,512]{1,0:T(8,128)S(1)}, f32[64,512]{1,0:T(8,128)S(1)}, u32[]{:S(2)}, u32[]{:S(2)}) collective-permute-start(f32[64,512]{1,0:T(8,128)S(1)} %collective-permute-done.2.refs_6_), channel_id=1, source_target_pairs={{0,64},{1,65},{2,66},{3,67},{4,68},{5,69},{6,70},{7,71},{8,72},{9,... | collective-permute-start | bytes 393224 | tf_op jit(solution)/shard_map/ppermute | solution.py:33
  59.6 1.3 %pad_maximum_fusion.panel = f32[576,512]{1,0:T(8,128)S(1)} fusion(f32[288,512]{1,0:T(8,128)} %collective-permute-done.18, f32[144,512]{1,0:T(8,128)} %copy-done.4, f32[72,512]{1,0:T(8,128)} %copy-done.3, f32[72,512]{1,0:T(8,128)} %copy-done.2), kind=kLoop, calls=%fused_computation | loop fusion | flops 884736 | bytes 2359296 | tf_op jit(solution)/shard_map/concatenate | solution.py:49
  60.9 1.7 %own_panel.1 = (bf16[512,1536]{1,0:T(8,128)(2,1)S(1)}, f32[1,512]{1,0:T(1,128)}, f32[8,128]{1,0:T(8,128)S(1)}) custom-call(s32[3]{0:T(128)S(1)} %pad_add_fusion.where, f32[576,512]{1,0:T(8,128)S(1)} %pad_maximum_fusion.panel), custom_call_target="tpu_custom_call" | custom-call | flops 1000 | bytes 1000 | tf_op jit(solution)/shard_map/own_panel/pallas_call | solution.py:185
  62.6 2.2 %copy-done = f32[512,2048]{1,0:T(8,128)S(1)} copy-done((f32[512,2048]{1,0:T(8,128)S(1)}, f32[512,2048]{1,0:T(8,128)}, u32[]{:S(2)}) %copy-start) | copy-done | bytes 4194328
  64.8 2.5 %cross_0.1.refs_13_ = f32[512,2048]{1,0:T(8,128)} custom-call(s32[3]{0:T(128)S(1)} %pad_add_fusion.where, f32[192,512]{1,0:T(8,128)S(1)} %constant_dynamic-update-slice_fusion.refs_0_, f32[320,512]{1,0:T(8,128)S(1)} %constant_dynamic-update-slice_fusion.3.refs_1_, bf16[512,1536]{1,0:T(8,128)(2,1)S(1)} %get-tuple-element.39.refs_2_.refs_10_, ...), custom_call_target="tpu_custom_call" | custom-call | flops 1000 | bytes 1000 | tf_op jit(solution)/shard_map/cross_0/pallas_call | solution.py:200
  67.3 0.7 collective-permute-done.15.refs_9_
  68.1 0.2 collective-permute-done.14.refs_8_
  68.3 0.0 collective-permute-done.13.refs_7_
  68.3 0.7 collective-permute-done.12.refs_3_
  69.0 0.0 collective-permute-done.11.refs_1_
  69.0 6.1 %cross_1_3_2.1 = f32[512,2048]{1,0:T(8,128)} custom-call(s32[3]{0:T(128)S(1)} %pad_add_fusion.where, f32[192,512]{1,0:T(8,128)S(1)} %collective-permute-done.6.refs_0_, f32[320,512]{1,0:T(8,128)S(1)} %collective-permute-done.11.refs_1_, f32[192,512]{1,0:T(8,128)S(1)} %collective-permute-done.7.refs_2_, ...), custom_call_target="tpu_custom_call", output_to_operand_aliasing={{}: (14, {})} | custom-call | flops 1000 | bytes 1000 | tf_op jit(solution)/shard_map/cross_1_3_2/pallas_call | solution.py:200
  (16 shorter events, 0.2 us)
Async XLA Ops:
  0.6 8.4 %collective-permute-start.3 = (f32[64,512]{1,0:T(8,128)}, f32[64,512]{1,0:T(8,128)S(1)}, u32[]{:S(2)}, u32[]{:S(2)}) collective-permute-start(f32[64,512]{1,0:T(8,128)} %param.5), channel_id=1, source_target_pairs={{0,0},{1,128},{2,32},{3,224},{4,64},{5,192},{6,96},{7,160},{8,8},{... | collective-permute-start | bytes 393224 | tf_op jit(solution)/shard_map/ppermute | solution.py:33
  4.4 15.5 %collective-permute-start = (f32[64,512]{1,0:T(8,128)}, f32[64,512]{1,0:T(8,128)S(1)}, u32[]{:S(2)}, u32[]{:S(2)}) collective-permute-start(f32[64,512]{1,0:T(8,128)} %param.5), channel_id=1, source_target_pairs={{0,16},{1,144},{2,48},{3,240},{4,80},{5,208},{6,112},{7,176},{8,24... | collective-permute-start | bytes 393224 | tf_op jit(solution)/shard_map/ppermute | solution.py:33
  8.1 34.3 %copy-start.2 = (f32[72,512]{1,0:T(8,128)}, f32[72,512]{1,0:T(8,128)S(1)}, u32[]{:S(2)}) copy-start(f32[72,512]{1,0:T(8,128)S(1)} %select_maximum_fusion) | copy-start | bytes 442372
  9.0 16.5 %collective-permute-start.5 = (f32[64,512]{1,0:T(8,128)S(1)}, f32[64,512]{1,0:T(8,128)S(1)}, u32[]{:S(2)}, u32[]{:S(2)}) collective-permute-start(f32[64,512]{1,0:T(8,128)S(1)} %collective-permute-done.3), channel_id=1, source_target_pairs={{0,64},{1,65},{2,66},{3,67},{4,68},{5,69},{6,70},{7,71},{8,72},{9,... | collective-permute-start | bytes 393224 | tf_op jit(solution)/shard_map/ppermute | solution.py:33
  14.1 11.7 %collective-permute-start.4 = (f32[64,512]{1,0:T(8,128)S(1)}, f32[64,512]{1,0:T(8,128)S(1)}, u32[]{:S(2)}, u32[]{:S(2)}) collective-permute-start(f32[64,512]{1,0:T(8,128)S(1)} %collective-permute-done.3), channel_id=1, source_target_pairs={{0,192},{1,193},{2,194},{3,195},{4,196},{5,197},{6,198},{7,199},{8... | collective-permute-start | bytes 393224 | tf_op jit(solution)/shard_map/ppermute | solution.py:33
  19.7 6.3 %collective-permute-start.16 = (f32[72,512]{1,0:T(8,128)S(1)}, f32[72,512]{1,0:T(8,128)S(1)}, u32[]{:S(2)}, u32[]{:S(2)}) collective-permute-start(f32[72,512]{1,0:T(8,128)S(1)} %select_maximum_fusion), channel_id=1, source_target_pairs={{0,2},{1,3},{2,0},{3,1},{4,6},{5,7},{6,4},{7,5},{8,10},{9,11},{10,... | collective-permute-start | bytes 442376 | tf_op jit(solution)/shard_map/ppermute | solution.py:33
  20.0 13.6 %collective-permute-start.2 = (f32[64,512]{1,0:T(8,128)S(1)}, f32[64,512]{1,0:T(8,128)S(1)}, u32[]{:S(2)}, u32[]{:S(2)}) collective-permute-start(f32[64,512]{1,0:T(8,128)S(1)} %collective-permute-done.refs_4_), channel_id=1, source_target_pairs={{0,64},{1,65},{2,66},{3,67},{4,68},{5,69},{6,70},{7,71},{8,72},{9,... | collective-permute-start | bytes 393224 | tf_op jit(solution)/shard_map/ppermute | solution.py:33
  20.0 19.1 %collective-permute-start.1 = (f32[64,512]{1,0:T(8,128)S(1)}, f32[64,512]{1,0:T(8,128)S(1)}, u32[]{:S(2)}, u32[]{:S(2)}) collective-permute-start(f32[64,512]{1,0:T(8,128)S(1)} %collective-permute-done.refs_4_), channel_id=1, source_target_pairs={{0,192},{1,193},{2,194},{3,195},{4,196},{5,197},{6,198},{7,199},{8... | collective-permute-start | bytes 393224 | tf_op jit(solution)/shard_map/ppermute | solution.py:33
  26.0 16.5 %copy-start.3 = (f32[72,512]{1,0:T(8,128)}, f32[72,512]{1,0:T(8,128)S(1)}, u32[]{:S(2)}) copy-start(f32[72,512]{1,0:T(8,128)S(1)} %collective-permute-done.16) | copy-start | bytes 442372
  26.0 13.1 %collective-permute-start.17 = (f32[144,512]{1,0:T(8,128)S(1)}, f32[144,512]{1,0:T(8,128)S(1)}, u32[]{:S(2)}, u32[]{:S(2)}) collective-permute-start(f32[144,512]{1,0:T(8,128)S(1)} %pad_maximum_fusion.6), channel_id=1, source_target_pairs={{0,4},{1,5},{2,6},{3,7},{4,0},{5,1},{6,2},{7,3},{8,12},{9,13},{10,... | collective-permute-start | bytes 884744 | tf_op jit(solution)/shard_map/ppermute | solution.py:33
  29.7 20.7 %collective-permute-start.7 = (f32[192,512]{1,0:T(8,128)S(1)}, f32[192,512]{1,0:T(8,128)S(1)}, u32[]{:S(2)}, u32[]{:S(2)}) collective-permute-start(f32[192,512]{1,0:T(8,128)S(1)} %constant_dynamic-update-slice_fusion.refs_0_), channel_id=1, source_target_pairs={{0,8},{1,9},{2,10},{3,11},{4,12},{5,13},{6,14},{7,15},{8,16},{9,17... | collective-permute-start | bytes 1179656 | tf_op jit(solution)/shard_map/ppermute | solution.py:33
  29.8 20.7 %collective-permute-start.6 = (f32[192,512]{1,0:T(8,128)S(1)}, f32[192,512]{1,0:T(8,128)S(1)}, u32[]{:S(2)}, u32[]{:S(2)}) collective-permute-start(f32[192,512]{1,0:T(8,128)S(1)} %constant_dynamic-update-slice_fusion.refs_0_), channel_id=1, source_target_pairs={{0,24},{1,25},{2,26},{3,27},{4,28},{5,29},{6,30},{7,31},{8,0},{9,1... | collective-permute-start | bytes 1179656 | tf_op jit(solution)/shard_map/ppermute | solution.py:33
  33.6 16.9 %collective-permute-start.9 = (f32[128,512]{1,0:T(8,128)S(1)}, f32[128,512]{1,0:T(8,128)S(1)}, u32[]{:S(2)}, u32[]{:S(2)}) collective-permute-start(f32[128,512]{1,0:T(8,128)S(1)} %get-tuple-element.44), channel_id=1, source_target_pairs={{0,32},{1,33},{2,34},{3,35},{4,36},{5,37},{6,38},{7,39},{8,40},{9,... | collective-permute-start | bytes 786440 | tf_op jit(solution)/shard_map/ppermute | solution.py:33
  39.1 11.3 %collective-permute-start.8 = (f32[128,512]{1,0:T(8,128)S(1)}, f32[128,512]{1,0:T(8,128)S(1)}, u32[]{:S(2)}, u32[]{:S(2)}) collective-permute-start(f32[128,512]{1,0:T(8,128)S(1)} %get-tuple-element.45), channel_id=1, source_target_pairs={{0,224},{1,225},{2,226},{3,227},{4,228},{5,229},{6,230},{7,231},{8... | collective-permute-start | bytes 786440 | tf_op jit(solution)/shard_map/ppermute | solution.py:33
  39.1 11.3 %copy-start.4 = (f32[144,512]{1,0:T(8,128)}, f32[144,512]{1,0:T(8,128)S(1)}, u32[]{:S(2)}) copy-start(f32[144,512]{1,0:T(8,128)S(1)} %collective-permute-done.17) | copy-start | bytes 884740
  39.1 11.3 %collective-permute-start.10 = (f32[64,512]{1,0:T(8,128)S(1)}, f32[64,512]{1,0:T(8,128)S(1)}, u32[]{:S(2)}, u32[]{:S(2)}) collective-permute-start(f32[64,512]{1,0:T(8,128)S(1)} %collective-permute-done.4), channel_id=1, source_target_pairs={{0,192},{1,193},{2,194},{3,195},{4,196},{5,197},{6,198},{7,199},{8... | collective-permute-start | bytes 393224 | tf_op jit(solution)/shard_map/ppermute | solution.py:33
  50.4 7.6 %collective-permute-start.18 = (f32[288,512]{1,0:T(8,128)}, f32[288,512]{1,0:T(8,128)}, u32[]{:S(2)}, u32[]{:S(2)}) collective-permute-start(f32[288,512]{1,0:T(8,128)} %pad_maximum_fusion.1), channel_id=1, source_target_pairs={{0,1},{1,0},{2,3},{3,2},{4,5},{5,4},{6,7},{7,6},{8,9},{9,8},{10,11... | collective-permute-start | bytes 1769480 | tf_op jit(solution)/shard_map/ppermute | solution.py:33
  50.5 18.4 %collective-permute-start.12 = (f32[320,512]{1,0:T(8,128)S(1)}, f32[320,512]{1,0:T(8,128)S(1)}, u32[]{:S(2)}, u32[]{:S(2)}) collective-permute-start(f32[320,512]{1,0:T(8,128)S(1)} %constant_dynamic-update-slice_fusion.3.refs_1_), channel_id=1, source_target_pairs={{0,8},{1,9},{2,10},{3,11},{4,12},{5,13},{6,14},{7,15},{8,16},{9,17... | collective-permute-start | bytes 1966088 | tf_op jit(solution)/shard_map/ppermute | solution.py:33
  50.8 18.2 %collective-permute-start.11 = (f32[320,512]{1,0:T(8,128)S(1)}, f32[320,512]{1,0:T(8,128)S(1)}, u32[]{:S(2)}, u32[]{:S(2)}) collective-permute-start(f32[320,512]{1,0:T(8,128)S(1)} %constant_dynamic-update-slice_fusion.3.refs_1_), channel_id=1, source_target_pairs={{0,24},{1,25},{2,26},{3,27},{4,28},{5,29},{6,30},{7,31},{8,0},{9,1... | collective-permute-start | bytes 1966088 | tf_op jit(solution)/shard_map/ppermute | solution.py:33
  54.7 13.5 %collective-permute-start.14 = (f32[128,512]{1,0:T(8,128)}, f32[128,512]{1,0:T(8,128)}, u32[]{:S(2)}, u32[]{:S(2)}) collective-permute-start(f32[128,512]{1,0:T(8,128)} %get-tuple-element.42), channel_id=1, source_target_pairs={{0,32},{1,33},{2,34},{3,35},{4,36},{5,37},{6,38},{7,39},{8,40},{9,... | collective-permute-start | bytes 786440 | tf_op jit(solution)/shard_map/ppermute | solution.py:33
  54.7 13.5 %collective-permute-start.13 = (f32[128,512]{1,0:T(8,128)}, f32[128,512]{1,0:T(8,128)}, u32[]{:S(2)}, u32[]{:S(2)}) collective-permute-start(f32[128,512]{1,0:T(8,128)} %get-tuple-element.43), channel_id=1, source_target_pairs={{0,224},{1,225},{2,226},{3,227},{4,228},{5,229},{6,230},{7,231},{8... | collective-permute-start | bytes 786440 | tf_op jit(solution)/shard_map/ppermute | solution.py:33
  58.1 10.0 %collective-permute-start.15 = (f32[64,512]{1,0:T(8,128)S(1)}, f32[64,512]{1,0:T(8,128)S(1)}, u32[]{:S(2)}, u32[]{:S(2)}) collective-permute-start(f32[64,512]{1,0:T(8,128)S(1)} %collective-permute-done.2.refs_6_), channel_id=1, source_target_pairs={{0,64},{1,65},{2,66},{3,67},{4,68},{5,69},{6,70},{7,71},{8,72},{9,... | collective-permute-start | bytes 393224 | tf_op jit(solution)/shard_map/ppermute | solution.py:33
  62.6 2.2 %copy-start = (f32[512,2048]{1,0:T(8,128)S(1)}, f32[512,2048]{1,0:T(8,128)}, u32[]{:S(2)}) copy-start(f32[512,2048]{1,0:T(8,128)} %refs_12_.1) | copy-start | bytes 12582916
  64.8 4.1 %copy-start.1 = (f32[512,2048]{1,0:T(8,128)S(1)}, f32[512,2048]{1,0:T(8,128)}, u32[]{:S(2)}) copy-start(f32[512,2048]{1,0:T(8,128)} %refs_12_.1) | copy-start | bytes 12582916

commit v3 on v2

--- a/solution.py
+++ b/solution.py
@@ -159,12 +159,13 @@
     ups, downs = fetch(join(shard, up), z=1), fetch(join(shard, down), z=-1)
     across = fetch(up, z=2)
     up_far, down_far = fetch(far, z=2), fetch(far, z=-2)
+    own, up_far, down_far = together((own, up_far, down_far))
+    own = join(own, swap(own, x=2))
     first = join(shard, up, down)
     near, back = fetch(first, y=1), fetch(first, y=3)
     up_far, down_far, near, back, ups, downs, across = together(
         (up_far, down_far, near, back, ups, downs, across)
     )
-    own = join(own, swap(own, x=2))
     own = join(own, swap(own, k=1))
     rest = join(ups, downs, across)
     near_rest, back_rest = fetch(rest, y=1), fetch(rest, y=3)

time: 75.9 us -> 80 us (1.054)
  waiting for transfers between devices: 10.9 us -> 19.1 us
  starting transfers between devices: 46.6 us -> 42.5 us
    ppermute x19, waiting for transfers between devices: 10.9 us -> 19.1 us  [permute(): return lax.ppermute(array, ('row', 'col'), pairs)]
    ppermute x19, starting transfers between devices: 46.6 us -> 42.5 us  [permute(): return lax.ppermute(array, ('row', 'col'), pairs)]
    unnamed x14 -> x12, local copies, waits for them, and re-layouts: 2.26 us -> 2.26 us
  transfers between devices with their start and end apart: 19 -> 19, of which waited for: 7 -> 8; matrix products, arithmetic and copies ran while one was open for 6% -> 5% of each run, Pallas kernels for 6% -> 5%
where the time goes in v3:
time: 80 us; the launch traced here: 79.1 us
  starting transfers between devices  42.5 us (53%)
  waiting for transfers between devices  19.1 us (24%)
  Pallas kernels  10.4 us (13%)
  other arithmetic  4.12 us (5%)
  local copies, waits for them, and re-layouts  2.28 us (3%)
    ppermute x19, starting transfers between devices, permute(): return lax.ppermute(array, ('row', 'col'), pairs)  42.5 us
    ppermute x19, waiting for transfers between devices, permute(): return lax.ppermute(array, ('row', 'col'), pairs)  19.1 us
    pallas_call x2, Pallas kernels, cross(): kernel(functools.partial(cross_kernel, counts=counts, which=which, diagon...  8.64 us
    concatenate x6, other arithmetic, join(): return jnp.concatenate(arrays, axis=0)  4.04 us
    unnamed x12, local copies, waits for them, and re-layouts  2.26 us
    pallas_call x1, Pallas kernels, per_device(): kernel(panel_kernel, (), [held], [held] * len(outs), outs, 'own_panel', [...  1.72 us
  transfers between devices with their start and end apart: 19, of which 8 were waited for; matrix products, arithmetic and copies ran while one was open for 5% of the time, Pallas kernels for 5%

profile of v3, /device:TPU:2, one launch (start us, length us, event | category | flops | bytes accessed | tf_op | source)
XLA Modules:
  0.0 79.1 jit_solution(3870653215833686094)
XLA Ops:
  0.6 3.8 %collective-permute-start = (f32[64,512]{1,0:T(8,128)}, f32[64,512]{1,0:T(8,128)S(1)}, u32[]{:S(2)}, u32[]{:S(2)}) collective-permute-start(f32[64,512]{1,0:T(8,128)} %param.5), channel_id=1, source_target_pairs={{0,0},{1,128},{2,32},{3,224},{4,64},{5,192},{6,96},{7,160},{8,8},{... | collective-permute-start | bytes 393224 | tf_op jit(solution)/shard_map/ppermute | solution.py:33
  4.4 2.7 %collective-permute-start.2 = (f32[64,512]{1,0:T(8,128)}, f32[64,512]{1,0:T(8,128)S(1)}, u32[]{:S(2)}, u32[]{:S(2)}) collective-permute-start(f32[64,512]{1,0:T(8,128)} %param.5), channel_id=1, source_target_pairs={{0,16},{1,144},{2,48},{3,240},{4,80},{5,208},{6,112},{7,176},{8,24... | collective-permute-start | bytes 393224 | tf_op jit(solution)/shard_map/ppermute | solution.py:33
  7.2 0.9 %select_maximum_fusion = f32[72,512]{1,0:T(8,128)S(1)} fusion(f32[1,64]{1,0:T(1,128)} %bitcast.5, f32[64,512]{1,0:T(8,128)} %param.5), kind=kLoop, calls=%fused_computation.7 | loop fusion | flops 110592 | bytes 278784 | tf_op jit(solution)/shard_map/concatenate | solution.py:49
  8.1 0.9 %collective-permute-done = f32[64,512]{1,0:T(8,128)S(1)} collective-permute-done((f32[64,512]{1,0:T(8,128)}, f32[64,512]{1,0:T(8,128)S(1)}, u32[]{:S(2)}, u32[]{:S(2)}) %collective-permute-start) | collective-permute-done | bytes 131104 | tf_op jit(solution)/shard_map/ppermute | solution.py:33
  9.0 5.0 %collective-permute-start.6 = (f32[64,512]{1,0:T(8,128)S(1)}, f32[64,512]{1,0:T(8,128)S(1)}, u32[]{:S(2)}, u32[]{:S(2)}) collective-permute-start(f32[64,512]{1,0:T(8,128)S(1)} %collective-permute-done), channel_id=1, source_target_pairs={{0,64},{1,65},{2,66},{3,67},{4,68},{5,69},{6,70},{7,71},{8,72},{9,... | collective-permute-start | bytes 393224 | tf_op jit(solution)/shard_map/ppermute | solution.py:33
  14.1 5.6 %collective-permute-start.5 = (f32[64,512]{1,0:T(8,128)S(1)}, f32[64,512]{1,0:T(8,128)S(1)}, u32[]{:S(2)}, u32[]{:S(2)}) collective-permute-start(f32[64,512]{1,0:T(8,128)S(1)} %collective-permute-done), channel_id=1, source_target_pairs={{0,192},{1,193},{2,194},{3,195},{4,196},{5,197},{6,198},{7,199},{8... | collective-permute-start | bytes 393224 | tf_op jit(solution)/shard_map/ppermute | solution.py:33
  19.7 0.2 collective-permute-start.1
  19.9 0.0 collective-permute-done.2.refs_4_
  20.0 0.1 collective-permute-start.4
  20.0 5.5 %collective-permute-start.3 = (f32[64,512]{1,0:T(8,128)S(1)}, f32[64,512]{1,0:T(8,128)S(1)}, u32[]{:S(2)}, u32[]{:S(2)}) collective-permute-start(f32[64,512]{1,0:T(8,128)S(1)} %collective-permute-done.2.refs_4_), channel_id=1, source_target_pairs={{0,192},{1,193},{2,194},{3,195},{4,196},{5,197},{6,198},{7,199},{8... | collective-permute-start | bytes 393224 | tf_op jit(solution)/shard_map/ppermute | solution.py:33
  25.6 0.0 collective-permute-done.6
  25.6 0.2 collective-permute-done.5
  25.8 0.2 collective-permute-done.1
  26.0 4.7 %collective-permute-done.4.refs_6_ = f32[64,512]{1,0:T(8,128)S(1)} collective-permute-done((f32[64,512]{1,0:T(8,128)S(1)}, f32[64,512]{1,0:T(8,128)S(1)}, u32[]{:S(2)}, u32[]{:S(2)}) %collective-permute-start.4) | collective-permute-done | bytes 131104 | tf_op jit(solution)/shard_map/ppermute | solution.py:33
  30.7 1.0 %collective-permute-done.3.refs_5_ = f32[64,512]{1,0:T(8,128)S(1)} collective-permute-done((f32[64,512]{1,0:T(8,128)S(1)}, f32[64,512]{1,0:T(8,128)S(1)}, u32[]{:S(2)}, u32[]{:S(2)}) %collective-permute-start.3) | collective-permute-done | bytes 131104 | tf_op jit(solution)/shard_map/ppermute | solution.py:33
  31.7 1.7 %collective-permute-start.17 = (f32[144,512]{1,0:T(8,128)S(1)}, f32[144,512]{1,0:T(8,128)S(1)}, u32[]{:S(2)}, u32[]{:S(2)}) collective-permute-start(f32[144,512]{1,0:T(8,128)S(1)} %pad_maximum_fusion.6), channel_id=1, source_target_pairs={{0,4},{1,5},{2,6},{3,7},{4,0},{5,1},{6,2},{7,3},{8,12},{9,13},{10,... | collective-permute-start | bytes 884744 | tf_op jit(solution)/shard_map/ppermute | solution.py:33
  33.5 2.1 %collective-permute-start.8 = (f32[192,512]{1,0:T(8,128)S(1)}, f32[192,512]{1,0:T(8,128)S(1)}, u32[]{:S(2)}, u32[]{:S(2)}) collective-permute-start(f32[192,512]{1,0:T(8,128)S(1)} %constant_dynamic-update-slice_fusion.refs_0_), channel_id=1, source_target_pairs={{0,8},{1,9},{2,10},{3,11},{4,12},{5,13},{6,14},{7,15},{8,16},{9,17... | collective-permute-start | bytes 1179656 | tf_op jit(solution)/shard_map/ppermute | solution.py:33
  35.6 3.6 %collective-permute-start.7 = (f32[192,512]{1,0:T(8,128)S(1)}, f32[192,512]{1,0:T(8,128)S(1)}, u32[]{:S(2)}, u32[]{:S(2)}) collective-permute-start(f32[192,512]{1,0:T(8,128)S(1)} %constant_dynamic-update-slice_fusion.refs_0_), channel_id=1, source_target_pairs={{0,24},{1,25},{2,26},{3,27},{4,28},{5,29},{6,30},{7,31},{8,0},{9,1... | collective-permute-start | bytes 1179656 | tf_op jit(solution)/shard_map/ppermute | solution.py:33
  39.3 1.8 %collective-permute-start.10 = (f32[128,512]{1,0:T(8,128)S(1)}, f32[128,512]{1,0:T(8,128)S(1)}, u32[]{:S(2)}, u32[]{:S(2)}) collective-permute-start(f32[128,512]{1,0:T(8,128)S(1)} %get-tuple-element.50), channel_id=1, source_target_pairs={{0,32},{1,33},{2,34},{3,35},{4,36},{5,37},{6,38},{7,39},{8,40},{9,... | collective-permute-start | bytes 786440 | tf_op jit(solution)/shard_map/ppermute | solution.py:33
  41.1 1.5 %collective-permute-start.9 = (f32[128,512]{1,0:T(8,128)S(1)}, f32[128,512]{1,0:T(8,128)S(1)}, u32[]{:S(2)}, u32[]{:S(2)}) collective-permute-start(f32[128,512]{1,0:T(8,128)S(1)} %get-tuple-element.51), channel_id=1, source_target_pairs={{0,224},{1,225},{2,226},{3,227},{4,228},{5,229},{6,230},{7,231},{8... | collective-permute-start | bytes 786440 | tf_op jit(solution)/shard_map/ppermute | solution.py:33
  42.6 0.0 collective-permute-done.17
  42.6 0.7 collective-permute-start.11
  43.3 0.9 %pad_maximum_fusion.1 = f32[288,512]{1,0:T(8,128)} fusion(f32[144,512]{1,0:T(8,128)S(1)} %collective-permute-done.17, f32[144,512]{1,0:T(8,128)S(1)} %pad_maximum_fusion.6), kind=kLoop, calls=%fused_computation.1 | loop fusion | flops 147456 | bytes 1179648 | tf_op jit(solution)/shard_map/concatenate | solution.py:49
  44.1 0.0 copy-done.2
  44.1 10.3 %collective-permute-done.11 = f32[64,512]{1,0:T(8,128)S(1)} collective-permute-done((f32[64,512]{1,0:T(8,128)S(1)}, f32[64,512]{1,0:T(8,128)S(1)}, u32[]{:S(2)}, u32[]{:S(2)}) %collective-permute-start.11) | collective-permute-done | bytes 131104 | tf_op jit(solution)/shard_map/ppermute | solution.py:33
  54.4 0.0 collective-permute-start.18
  54.4 0.0 collective-permute-done.10
  54.4 0.0 collective-permute-done.9
  54.5 0.0 collective-permute-done.8.refs_2_
  54.5 0.0 collective-permute-done.7.refs_0_
  54.6 0.3 collective-permute-start.13
  54.9 3.0 %collective-permute-start.12 = (f32[320,512]{1,0:T(8,128)S(1)}, f32[320,512]{1,0:T(8,128)S(1)}, u32[]{:S(2)}, u32[]{:S(2)}) collective-permute-start(f32[320,512]{1,0:T(8,128)S(1)} %constant_dynamic-update-slice_fusion.3.refs_1_), channel_id=1, source_target_pairs={{0,24},{1,25},{2,26},{3,27},{4,28},{5,29},{6,30},{7,31},{8,0},{9,1... | collective-permute-start | bytes 1966088 | tf_op jit(solution)/shard_map/ppermute | solution.py:33
  57.9 0.9 %pad_maximum_fusion.4 = (f32[128,512]{1,0:T(8,128)}, f32[128,512]{1,0:T(8,128)}) fusion(f32[64,512]{1,0:T(8,128)S(1)} %collective-permute-done.2.refs_4_, f32[64,512]{1,0:T(8,128)S(1)} %collective-permute-done.4.refs_6_, f32[64,512]{1,0:T(8,128)S(1)} %collective-permute-done.3.refs_5_), kind=kLoop, calls=%fused_computation.4 | loop fusion | flops 131072 | bytes 917504 | tf_op jit(solution)/shard_map/concatenate | solution.py:49
  58.7 0.0 collective-permute-start.15
  58.7 3.2 %collective-permute-start.14 = (f32[128,512]{1,0:T(8,128)}, f32[128,512]{1,0:T(8,128)}, u32[]{:S(2)}, u32[]{:S(2)}) collective-permute-start(f32[128,512]{1,0:T(8,128)} %get-tuple-element.49), channel_id=1, source_target_pairs={{0,224},{1,225},{2,226},{3,227},{4,228},{5,229},{6,230},{7,231},{8... | collective-permute-start | bytes 786440 | tf_op jit(solution)/shard_map/ppermute | solution.py:33
  62.0 0.1 pad_add_fusion.where
  62.0 0.0 collective-permute-done.18
  62.1 1.5 %collective-permute-start.16 = (f32[64,512]{1,0:T(8,128)S(1)}, f32[64,512]{1,0:T(8,128)S(1)}, u32[]{:S(2)}, u32[]{:S(2)}) collective-permute-start(f32[64,512]{1,0:T(8,128)S(1)} %collective-permute-done.4.refs_6_), channel_id=1, source_target_pairs={{0,64},{1,65},{2,66},{3,67},{4,68},{5,69},{6,70},{7,71},{8,72},{9,... | collective-permute-start | bytes 393224 | tf_op jit(solution)/shard_map/ppermute | solution.py:33
  63.6 1.3 %pad_maximum_fusion.panel = f32[576,512]{1,0:T(8,128)S(1)} fusion(f32[288,512]{1,0:T(8,128)} %collective-permute-done.18, f32[144,512]{1,0:T(8,128)} %copy-done.3, f32[144,512]{1,0:T(8,128)} %copy-done.2), kind=kLoop, calls=%fused_computation | loop fusion | flops 589824 | bytes 2359296 | tf_op jit(solution)/shard_map/concatenate | solution.py:49
  64.9 1.7 %own_panel.1 = (bf16[512,1536]{1,0:T(8,128)(2,1)S(1)}, f32[1,512]{1,0:T(1,128)}, f32[8,128]{1,0:T(8,128)S(1)}) custom-call(s32[3]{0:T(128)S(1)} %pad_add_fusion.where, f32[576,512]{1,0:T(8,128)S(1)} %pad_maximum_fusion.panel), custom_call_target="tpu_custom_call" | custom-call | flops 1000 | bytes 1000 | tf_op jit(solution)/shard_map/own_panel/pallas_call | solution.py:186
  66.6 2.2 %copy-done = f32[512,2048]{1,0:T(8,128)S(1)} copy-done((f32[512,2048]{1,0:T(8,128)S(1)}, f32[512,2048]{1,0:T(8,128)}, u32[]{:S(2)}) %copy-start) | copy-done | bytes 4194328
  68.8 2.5 %cross_0.1.refs_13_ = f32[512,2048]{1,0:T(8,128)} custom-call(s32[3]{0:T(128)S(1)} %pad_add_fusion.where, f32[192,512]{1,0:T(8,128)S(1)} %constant_dynamic-update-slice_fusion.refs_0_, f32[320,512]{1,0:T(8,128)S(1)} %constant_dynamic-update-slice_fusion.3.refs_1_, bf16[512,1536]{1,0:T(8,128)(2,1)S(1)} %get-tuple-element.45.refs_2_.refs_10_, ...), custom_call_target="tpu_custom_call" | custom-call | flops 1000 | bytes 1000 | tf_op jit(solution)/shard_map/cross_0/pallas_call | solution.py:201
  71.3 0.0 collective-permute-done.16.refs_9_
  71.3 0.9 %collective-permute-done.15.refs_8_ = f32[128,512]{1,0:T(8,128)} collective-permute-done((f32[128,512]{1,0:T(8,128)}, f32[128,512]{1,0:T(8,128)}, u32[]{:S(2)}, u32[]{:S(2)}) %collective-permute-start.15) | collective-permute-done | bytes 262176 | tf_op jit(solution)/shard_map/ppermute | solution.py:33
  72.2 0.0 collective-permute-done.14.refs_7_
  72.3 0.7 collective-permute-done.13.refs_3_
  73.0 0.0 collective-permute-done.12.refs_1_
  73.0 6.1 %cross_1_3_2.1 = f32[512,2048]{1,0:T(8,128)} custom-call(s32[3]{0:T(128)S(1)} %pad_add_fusion.where, f32[192,512]{1,0:T(8,128)S(1)} %collective-permute-done.7.refs_0_, f32[320,512]{1,0:T(8,128)S(1)} %collective-permute-done.12.refs_1_, f32[192,512]{1,0:T(8,128)S(1)} %collective-permute-done.8.refs_2_, ...), custom_call_target="tpu_custom_call", output_to_operand_aliasing={{}: (14, {})} | custom-call | flops 1000 | bytes 1000 | tf_op jit(solution)/shard_map/cross_1_3_2/pallas_call | solution.py:201
  (14 shorter events, 0.2 us)
Async XLA Ops:
  0.6 8.4 %collective-permute-start = (f32[64,512]{1,0:T(8,128)}, f32[64,512]{1,0:T(8,128)S(1)}, u32[]{:S(2)}, u32[]{:S(2)}) collective-permute-start(f32[64,512]{1,0:T(8,128)} %param.5), channel_id=1, source_target_pairs={{0,0},{1,128},{2,32},{3,224},{4,64},{5,192},{6,96},{7,160},{8,8},{... | collective-permute-start | bytes 393224 | tf_op jit(solution)/shard_map/ppermute | solution.py:33
  4.4 15.5 %collective-permute-start.2 = (f32[64,512]{1,0:T(8,128)}, f32[64,512]{1,0:T(8,128)S(1)}, u32[]{:S(2)}, u32[]{:S(2)}) collective-permute-start(f32[64,512]{1,0:T(8,128)} %param.5), channel_id=1, source_target_pairs={{0,16},{1,144},{2,48},{3,240},{4,80},{5,208},{6,112},{7,176},{8,24... | collective-permute-start | bytes 393224 | tf_op jit(solution)/shard_map/ppermute | solution.py:33
  9.0 16.5 %collective-permute-start.6 = (f32[64,512]{1,0:T(8,128)S(1)}, f32[64,512]{1,0:T(8,128)S(1)}, u32[]{:S(2)}, u32[]{:S(2)}) collective-permute-start(f32[64,512]{1,0:T(8,128)S(1)} %collective-permute-done), channel_id=1, source_target_pairs={{0,64},{1,65},{2,66},{3,67},{4,68},{5,69},{6,70},{7,71},{8,72},{9,... | collective-permute-start | bytes 393224 | tf_op jit(solution)/shard_map/ppermute | solution.py:33
  14.1 11.7 %collective-permute-start.5 = (f32[64,512]{1,0:T(8,128)S(1)}, f32[64,512]{1,0:T(8,128)S(1)}, u32[]{:S(2)}, u32[]{:S(2)}) collective-permute-start(f32[64,512]{1,0:T(8,128)S(1)} %collective-permute-done), channel_id=1, source_target_pairs={{0,192},{1,193},{2,194},{3,195},{4,196},{5,197},{6,198},{7,199},{8... | collective-permute-start | bytes 393224 | tf_op jit(solution)/shard_map/ppermute | solution.py:33
  19.7 6.3 %collective-permute-start.1 = (f32[72,512]{1,0:T(8,128)S(1)}, f32[72,512]{1,0:T(8,128)S(1)}, u32[]{:S(2)}, u32[]{:S(2)}) collective-permute-start(f32[72,512]{1,0:T(8,128)S(1)} %select_maximum_fusion), channel_id=1, source_target_pairs={{0,2},{1,3},{2,0},{3,1},{4,6},{5,7},{6,4},{7,5},{8,10},{9,11},{10,... | collective-permute-start | bytes 442376 | tf_op jit(solution)/shard_map/ppermute | solution.py:33
  20.0 10.8 %collective-permute-start.4 = (f32[64,512]{1,0:T(8,128)S(1)}, f32[64,512]{1,0:T(8,128)S(1)}, u32[]{:S(2)}, u32[]{:S(2)}) collective-permute-start(f32[64,512]{1,0:T(8,128)S(1)} %collective-permute-done.2.refs_4_), channel_id=1, source_target_pairs={{0,64},{1,65},{2,66},{3,67},{4,68},{5,69},{6,70},{7,71},{8,72},{9,... | collective-permute-start | bytes 393224 | tf_op jit(solution)/shard_map/ppermute | solution.py:33
  20.0 11.7 %collective-permute-start.3 = (f32[64,512]{1,0:T(8,128)S(1)}, f32[64,512]{1,0:T(8,128)S(1)}, u32[]{:S(2)}, u32[]{:S(2)}) collective-permute-start(f32[64,512]{1,0:T(8,128)S(1)} %collective-permute-done.2.refs_4_), channel_id=1, source_target_pairs={{0,192},{1,193},{2,194},{3,195},{4,196},{5,197},{6,198},{7,199},{8... | collective-permute-start | bytes 393224 | tf_op jit(solution)/shard_map/ppermute | solution.py:33
  26.0 18.2 %copy-start.2 = (f32[144,512]{1,0:T(8,128)}, f32[144,512]{1,0:T(8,128)S(1)}, u32[]{:S(2)}) copy-start(f32[144,512]{1,0:T(8,128)S(1)} %pad_maximum_fusion.6) | copy-start | bytes 884740
  31.7 10.8 %collective-permute-start.17 = (f32[144,512]{1,0:T(8,128)S(1)}, f32[144,512]{1,0:T(8,128)S(1)}, u32[]{:S(2)}, u32[]{:S(2)}) collective-permute-start(f32[144,512]{1,0:T(8,128)S(1)} %pad_maximum_fusion.6), channel_id=1, source_target_pairs={{0,4},{1,5},{2,6},{3,7},{4,0},{5,1},{6,2},{7,3},{8,12},{9,13},{10,... | collective-permute-start | bytes 884744 | tf_op jit(solution)/shard_map/ppermute | solution.py:33
  33.5 21.0 %collective-permute-start.8 = (f32[192,512]{1,0:T(8,128)S(1)}, f32[192,512]{1,0:T(8,128)S(1)}, u32[]{:S(2)}, u32[]{:S(2)}) collective-permute-start(f32[192,512]{1,0:T(8,128)S(1)} %constant_dynamic-update-slice_fusion.refs_0_), channel_id=1, source_target_pairs={{0,8},{1,9},{2,10},{3,11},{4,12},{5,13},{6,14},{7,15},{8,16},{9,17... | collective-permute-start | bytes 1179656 | tf_op jit(solution)/shard_map/ppermute | solution.py:33
  35.6 18.9 %collective-permute-start.7 = (f32[192,512]{1,0:T(8,128)S(1)}, f32[192,512]{1,0:T(8,128)S(1)}, u32[]{:S(2)}, u32[]{:S(2)}) collective-permute-start(f32[192,512]{1,0:T(8,128)S(1)} %constant_dynamic-update-slice_fusion.refs_0_), channel_id=1, source_target_pairs={{0,24},{1,25},{2,26},{3,27},{4,28},{5,29},{6,30},{7,31},{8,0},{9,1... | collective-permute-start | bytes 1179656 | tf_op jit(solution)/shard_map/ppermute | solution.py:33
  39.3 15.2 %collective-permute-start.10 = (f32[128,512]{1,0:T(8,128)S(1)}, f32[128,512]{1,0:T(8,128)S(1)}, u32[]{:S(2)}, u32[]{:S(2)}) collective-permute-start(f32[128,512]{1,0:T(8,128)S(1)} %get-tuple-element.50), channel_id=1, source_target_pairs={{0,32},{1,33},{2,34},{3,35},{4,36},{5,37},{6,38},{7,39},{8,40},{9,... | collective-permute-start | bytes 786440 | tf_op jit(solution)/shard_map/ppermute | solution.py:33
  41.1 13.4 %collective-permute-start.9 = (f32[128,512]{1,0:T(8,128)S(1)}, f32[128,512]{1,0:T(8,128)S(1)}, u32[]{:S(2)}, u32[]{:S(2)}) collective-permute-start(f32[128,512]{1,0:T(8,128)S(1)} %get-tuple-element.51), channel_id=1, source_target_pairs={{0,224},{1,225},{2,226},{3,227},{4,228},{5,229},{6,230},{7,231},{8... | collective-permute-start | bytes 786440 | tf_op jit(solution)/shard_map/ppermute | solution.py:33
  42.6 11.9 %copy-start.3 = (f32[144,512]{1,0:T(8,128)}, f32[144,512]{1,0:T(8,128)S(1)}, u32[]{:S(2)}) copy-start(f32[144,512]{1,0:T(8,128)S(1)} %collective-permute-done.17) | copy-start | bytes 884740
  42.6 11.9 %collective-permute-start.11 = (f32[64,512]{1,0:T(8,128)S(1)}, f32[64,512]{1,0:T(8,128)S(1)}, u32[]{:S(2)}, u32[]{:S(2)}) collective-permute-start(f32[64,512]{1,0:T(8,128)S(1)} %collective-permute-done.5), channel_id=1, source_target_pairs={{0,192},{1,193},{2,194},{3,195},{4,196},{5,197},{6,198},{7,199},{8... | collective-permute-start | bytes 393224 | tf_op jit(solution)/shard_map/ppermute | solution.py:33
  54.4 7.6 %collective-permute-start.18 = (f32[288,512]{1,0:T(8,128)}, f32[288,512]{1,0:T(8,128)}, u32[]{:S(2)}, u32[]{:S(2)}) collective-permute-start(f32[288,512]{1,0:T(8,128)} %pad_maximum_fusion.1), channel_id=1, source_target_pairs={{0,1},{1,0},{2,3},{3,2},{4,5},{5,4},{6,7},{7,6},{8,9},{9,8},{10,11... | collective-permute-start | bytes 1769480 | tf_op jit(solution)/shard_map/ppermute | solution.py:33
  54.6 18.4 %collective-permute-start.13 = (f32[320,512]{1,0:T(8,128)S(1)}, f32[320,512]{1,0:T(8,128)S(1)}, u32[]{:S(2)}, u32[]{:S(2)}) collective-permute-start(f32[320,512]{1,0:T(8,128)S(1)} %constant_dynamic-update-slice_fusion.3.refs_1_), channel_id=1, source_target_pairs={{0,8},{1,9},{2,10},{3,11},{4,12},{5,13},{6,14},{7,15},{8,16},{9,17... | collective-permute-start | bytes 1966088 | tf_op jit(solution)/shard_map/ppermute | solution.py:33
  54.9 18.1 %collective-permute-start.12 = (f32[320,512]{1,0:T(8,128)S(1)}, f32[320,512]{1,0:T(8,128)S(1)}, u32[]{:S(2)}, u32[]{:S(2)}) collective-permute-start(f32[320,512]{1,0:T(8,128)S(1)} %constant_dynamic-update-slice_fusion.3.refs_1_), channel_id=1, source_target_pairs={{0,24},{1,25},{2,26},{3,27},{4,28},{5,29},{6,30},{7,31},{8,0},{9,1... | collective-permute-start | bytes 1966088 | tf_op jit(solution)/shard_map/ppermute | solution.py:33
  58.7 13.5 %collective-permute-start.15 = (f32[128,512]{1,0:T(8,128)}, f32[128,512]{1,0:T(8,128)}, u32[]{:S(2)}, u32[]{:S(2)}) collective-permute-start(f32[128,512]{1,0:T(8,128)} %get-tuple-element.48), channel_id=1, source_target_pairs={{0,32},{1,33},{2,34},{3,35},{4,36},{5,37},{6,38},{7,39},{8,40},{9,... | collective-permute-start | bytes 786440 | tf_op jit(solution)/shard_map/ppermute | solution.py:33
  58.7 13.5 %collective-permute-start.14 = (f32[128,512]{1,0:T(8,128)}, f32[128,512]{1,0:T(8,128)}, u32[]{:S(2)}, u32[]{:S(2)}) collective-permute-start(f32[128,512]{1,0:T(8,128)} %get-tuple-element.49), channel_id=1, source_target_pairs={{0,224},{1,225},{2,226},{3,227},{4,228},{5,229},{6,230},{7,231},{8... | collective-permute-start | bytes 786440 | tf_op jit(solution)/shard_map/ppermute | solution.py:33
  62.1 9.3 %collective-permute-start.16 = (f32[64,512]{1,0:T(8,128)S(1)}, f32[64,512]{1,0:T(8,128)S(1)}, u32[]{:S(2)}, u32[]{:S(2)}) collective-permute-start(f32[64,512]{1,0:T(8,128)S(1)} %collective-permute-done.4.refs_6_), channel_id=1, source_target_pairs={{0,64},{1,65},{2,66},{3,67},{4,68},{5,69},{6,70},{7,71},{8,72},{9,... | collective-permute-start | bytes 393224 | tf_op jit(solution)/shard_map/ppermute | solution.py:33
  66.6 2.2 %copy-start = (f32[512,2048]{1,0:T(8,128)S(1)}, f32[512,2048]{1,0:T(8,128)}, u32[]{:S(2)}) copy-start(f32[512,2048]{1,0:T(8,128)} %refs_12_.1) | copy-start | bytes 12582916
  68.8 4.2 %copy-start.1 = (f32[512,2048]{1,0:T(8,128)S(1)}, f32[512,2048]{1,0:T(8,128)}, u32[]{:S(2)}) copy-start(f32[512,2048]{1,0:T(8,128)} %refs_12_.1) | copy-start | bytes 12582916
